TPU v7x, 256 devices: a whole 4x4x8 slice. The times are simulated.
256 devices in a mesh: section: 32 (over x, z_hi, core), tensor: 8 (over y, z_lo).
Axes of the slice: x: 4, y: 4, z: 8 (z_hi: 4, z_lo: 2; z = z_hi * 2 + z_lo), core: 2. Of those that a mesh axis runs over, the one named last changes fastest.
Arguments:
- act_in: bfloat16 [32, 128, 4096], P('section', None, 'tensor'), may hold values from -6 to 6
- grad_in: bfloat16 [32, 128, 4096], P('section', None, 'tensor'), may hold values from -6 to 6
- held_stash: bfloat16 [32, 2, 128, 4096], P('section', None, None, 'tensor'), may hold values from -6 to 6
- new_batch: bfloat16 [128, 4096], P(None, 'tensor'), may hold values from -6 to 6
- head_grad: bfloat16 [128, 4096], P(None, 'tensor'), may hold values from -6 to 6
- norm_gain: float32 [32, 4096], P('section'), may hold values from 0.1 to 1.9
- w_query: bfloat16 [32, 4096, 4096], P('section', None, 'tensor'), may hold values from -0.09375 to 0.09375
- w_key: bfloat16 [32, 4096, 1024], P('section', None, 'tensor'), may hold values from -0.09375 to 0.09375
- w_value: bfloat16 [32, 4096, 1024], P('section', None, 'tensor'), may hold values from -0.09375 to 0.09375
- w_out: bfloat16 [32, 4096, 4096], P('section', 'tensor'), may hold values from -0.09375 to 0.09375
Outputs:
- act_out: bfloat16 [32, 2, 128, 4096], P('section', None, None, 'tensor')
- grad_out: bfloat16 [32, 2, 128, 4096], P('section', None, None, 'tensor')
All inputs are finite; a program needn't handle non-finite values.
Results may differ from a plain program's by a relative error of at most 0.019.
Values may be sent and summed in bfloat16 or wider, within the bound.
A program may use at most 128 MiB of HBM per device.

v0:
```python
import jax
import jax.numpy as jnp
from jax import lax
from jax.sharding import PartitionSpec as P

HD = 128


norm_eps = 1e-05


def from_behind(x, axis, by):
    devices = lax.axis_size(axis)
    return lax.ppermute(x, axis, [(i, (i + by) % devices) for i in range(devices)])


def shifted(block, axis, distance):
    devices = range(lax.axis_size(axis))
    route = [(i - distance, i) for i in devices if i - distance in devices]
    return lax.ppermute(block, axis, route)


def attend(query, keys, values):
    n_rows = query.shape[0]
    kv_local = keys.shape[1] // HD
    groups = query.shape[1] // keys.shape[1]
    query_four = query.reshape(n_rows, kv_local, groups, HD)
    keys_three = keys.reshape(n_rows, kv_local, HD)
    values_three = values.reshape(n_rows, kv_local, HD)
    scores = jnp.einsum(
        "tkgd,ukd->kgtu", query_four, keys_three, precision=lax.Precision.HIGHEST
    ) * HD ** (-0.5)
    causal = jnp.arange(n_rows)[:, None] >= jnp.arange(n_rows)[None, :]
    scores = jnp.where(causal, scores, -1e30)
    peak = jnp.max(scores, axis=-1, keepdims=True)
    expo = jnp.exp(scores - peak)
    probs = expo / jnp.sum(expo, axis=-1, keepdims=True)
    mixed = jnp.einsum("kgtu,ukd->tkgd", probs, values_three, precision=lax.Precision.HIGHEST)
    return mixed.reshape(n_rows, -1)


def rms_norm(hidden, gain_row):
    x_float = hidden.astype(jnp.float32)
    inv_rms = lax.rsqrt(jnp.mean(x_float * x_float, axis=-1, keepdims=True) + norm_eps)
    normed = (x_float * inv_rms * gain_row).astype(jnp.bfloat16)
    return (normed, inv_rms)


def project_in(normed, w_query, w_key, w_value):
    query = jnp.dot(normed, w_query, preferred_element_type=jnp.float32)
    keys = jnp.dot(normed, w_key, preferred_element_type=jnp.float32)
    values = jnp.dot(normed, w_value, preferred_element_type=jnp.float32)
    return (query, keys, values)


def group_partial(normed, w_query, w_key, w_value, w_out):
    query, keys, values = project_in(normed, w_query, w_key, w_value)
    mixed = attend(query, keys, values)
    return jnp.dot(mixed.astype(jnp.bfloat16), w_out, preferred_element_type=jnp.float32)


def group_backward(normed, grad_full, w_query, w_key, w_value, w_out):
    query, keys, values = project_in(normed, w_query, w_key, w_value)
    d_mixed = jnp.dot(grad_full, w_out.T, preferred_element_type=jnp.float32)
    unused, pullback = jax.vjp(attend, query, keys, values)
    d_query, d_keys, d_values = pullback(d_mixed)
    total = jnp.dot(d_query.astype(jnp.bfloat16), w_query.T, preferred_element_type=jnp.float32)
    total = total + jnp.dot(
        d_keys.astype(jnp.bfloat16), w_key.T, preferred_element_type=jnp.float32
    )
    return total + jnp.dot(
        d_values.astype(jnp.bfloat16), w_value.T, preferred_element_type=jnp.float32
    )


def norm_step(x_float, inv_rms, scaled, row_total, grad_float, full_width):
    result = (
        grad_float
        + inv_rms * scaled
        - x_float * (inv_rms * inv_rms * inv_rms) * row_total / full_width
    )
    return result.astype(jnp.bfloat16)


def per_device(
    act_in, grad_in, held_stash, new_batch, head_grad, norm_gain, w_query, w_key, w_value, w_out
):
    n_section = lax.axis_size("section")
    my_section = lax.axis_index("section")
    slice_width = act_in.shape[-1]
    column = lax.axis_index("tensor") * slice_width
    n_ticks = held_stash.shape[1]
    n_rows = act_in.shape[1]
    at_first = my_section == 0
    at_last = my_section == n_section - 1
    gain_row = norm_gain[0]
    full_width = gain_row.shape[0]
    query_w = w_query[0]
    key_w = w_key[0]
    value_w = w_value[0]
    out_w = w_out[0]
    recalled = from_behind(
        held_stash[0].reshape(n_ticks * n_rows, slice_width), "section", n_section // 2
    )
    start_act, start_grad, stash_full, fresh_full, head_full = (
        lax.all_gather(act_in[0], "tensor", axis=1, tiled=True),
        lax.all_gather(grad_in[0], "tensor", axis=1, tiled=True),
        lax.all_gather(recalled, "tensor", axis=1, tiled=True),
        lax.all_gather(new_batch, "tensor", axis=1, tiled=True),
        lax.all_gather(head_grad, "tensor", axis=1, tiled=True),
    )
    forward_list = []
    current = start_act
    for tick_num in range(n_ticks):
        normed, inv_rms = rms_norm(current, gain_row)
        partial_value = group_partial(normed, query_w, key_w, value_w, out_w)
        attention = lax.psum(partial_value.astype(jnp.bfloat16), "tensor").astype(jnp.float32)
        layer_out = (current.astype(jnp.float32) + attention).astype(jnp.bfloat16)
        forward_list.append(lax.dynamic_slice_in_dim(layer_out, column, slice_width, 1))
        if tick_num + 1 < n_ticks:
            arrived = shifted(layer_out, "section", 1)
            current = jnp.where(at_first, fresh_full, arrived)
    backward_list = []
    grad_now = start_grad
    for tick_num in range(n_ticks):
        stashed = stash_full[tick_num * n_rows : (tick_num + 1) * n_rows]
        normed, inv_rms = rms_norm(stashed, gain_row)
        d_part = group_backward(normed, grad_now, query_w, key_w, value_w, out_w)
        d_norm = lax.psum(d_part.astype(jnp.bfloat16), "tensor").astype(jnp.float32)
        x_float = stashed.astype(jnp.float32)
        scaled = d_norm * gain_row
        row_total = jnp.sum(scaled * x_float, axis=-1, keepdims=True)
        layer_grad = norm_step(
            x_float, inv_rms, scaled, row_total, grad_now.astype(jnp.float32), full_width
        )
        backward_list.append(lax.dynamic_slice_in_dim(layer_grad, column, slice_width, 1))
        if tick_num + 1 < n_ticks:
            arrived = shifted(layer_grad, "section", -1)
            grad_now = jnp.where(at_last, head_full, arrived)
    return (jnp.stack(forward_list, axis=0)[None], jnp.stack(backward_list, axis=0)[None])


def solution(mesh):
    in_specs = (
        P("section", None, "tensor"),
        P("section", None, "tensor"),
        P("section", None, None, "tensor"),
        P(None, "tensor"),
        P(None, "tensor"),
        P("section", None),
        P("section", None, "tensor"),
        P("section", None, "tensor"),
        P("section", None, "tensor"),
        P("section", "tensor", None),
    )
    out_specs = (P("section", None, None, "tensor"), P("section", None, None, "tensor"))
    return jax.shard_map(
        per_device, mesh=mesh, in_specs=in_specs, out_specs=out_specs, check_vma=False
    )
```

profile of v0, /device:TPU:8, one launch (start us, length us, event | category | flops | bytes accessed | tf_op | source)
XLA Modules:
  0.0 513.3 jit_solution(6379277053478494664)
XLA Ops:
  8.7 3.1 collective-permute-start.1
  11.8 6.7 %collective-permute-done.1 = bf16[256,512]{1,0:T(8,128)(2,1)S(1)} collective-permute-done((bf16[256,512]{1,0:T(8,128)(2,1)}, bf16[256,512]{1,0:T(8,128)(2,1)S(1)}, u32[]{:S(2)}, u32[]{:S(2)}) %collective-permute-start.1) | collective-permute-done | bytes 262176 | tf_op jit(solution)/shard_map/ppermute | solution.py:14
  19.3 6.4 %copy.37 = bf16[512,4096]{1,0:T(8,128)(2,1)} copy(bf16[512,4096]{0,1:T(8,128)(2,1)} %bitcast.258) | data formatting | bytes 8388608 | tf_op jit(solution)/shard_map/reshape.192
  25.8 28.7 %all-gather.14.cloned.1.call-done = bf16[1,128,4096]{2,1,0:T(8,128)(2,1)} async-done(((bf16[1,128,512]{2,1,0:T(8,128)(2,1)}), bf16[1,128,4096]{2,1,0:T(8,128)(2,1)}) %all-gather.14.cloned.1.call-update) | async-done | bytes 1048592 | tf_op jit(solution)/shard_map/all_gather | solution.py:106
  54.5 1.6 fusion.8
  56.1 1.7 convolution_bitcast_fusion.8
  57.9 3.8 fusion.42
  63.9 1.7 convolution_convert_fusion.1
  65.6 32.7 %all-gather.16.cloned.1.call-done = bf16[1,128,4096]{2,1,0:T(8,128)(2,1)} async-done(((bf16[1,128,512]{2,1,0:T(8,128)(2,1)}), bf16[1,128,4096]{2,1,0:T(8,128)(2,1)}) %all-gather.16.cloned.1.call-update) | async-done | bytes 1048592 | tf_op jit(solution)/shard_map/all_gather | solution.py:107
  98.3 4.0 convolution_bitcast_fusion.1
  102.4 51.6 %all-gather.10.cloned.1.call-done = bf16[256,4096]{1,0:T(8,128)(2,1)} async-done(((bf16[256,512]{1,0:T(8,128)(2,1)}), bf16[256,4096]{1,0:T(8,128)(2,1)}) %all-gather.10.cloned.1.call-update) | async-done | bytes 2097168 | tf_op jit(solution)/shard_map/all_gather | solution.py:108
  154.0 1.5 fusion.12
  155.5 4.2 fusion.37
  163.5 1.5 fusion.4
  165.4 1.5 fusion
  168.3 108.5 %all-reduce.7.cloned.1.call-done = (bf16[128,4096]{1,0:T(8,128)(2,1)}, bf16[128,4096]{1,0:T(8,128)(2,1)}) async-done(((bf16[128,4096]{1,0:T(8,128)(2,1)}, bf16[128,4096]{1,0:T(8,128)(2,1)}), (bf16[128,4096]{1,0:T(8,128)(2,1)}, bf16[128,4096]{1,0:T(8,128)(2,1)})) %all-reduce.7.cloned.1.call-update) | async-done | bytes 2097168 | tf_op jit(solution)/shard_map/psum | solution.py:117
  276.9 2.0 fusion.19
  278.9 1.9 fusion.18
  283.9 4.0 collective-permute-start
  287.9 1.5 fusion.34
  291.4 41.8 %all-gather.12.cloned.1.call-done = bf16[128,4096]{1,0:T(8,128)(2,1)} async-done(((bf16[128,512]{1,0:T(8,128)(2,1)}), bf16[128,4096]{1,0:T(8,128)(2,1)}) %all-gather.12.cloned.1.call-update) | async-done | bytes 1048592 | tf_op jit(solution)/shard_map/all_gather | solution.py:110
  334.5 4.2 convolution_bitcast_fusion
  339.8 1.8 fusion.32
  342.1 36.3 %all-gather.8.cloned.1.call-done = bf16[128,4096]{1,0:T(8,128)(2,1)} async-done(((bf16[128,512]{1,0:T(8,128)(2,1)}), bf16[128,4096]{1,0:T(8,128)(2,1)}) %all-gather.8.cloned.1.call-update) | async-done | bytes 1048592 | tf_op jit(solution)/shard_map/all_gather | solution.py:109
  378.4 1.7 multiply_reduce_fusion.2
  380.2 4.1 fusion.40
  386.5 1.5 fusion.6
  388.9 1.7 convolution_convert_fusion
  392.9 1.6 slice_convert_fusion
  396.3 1.5 convert_element_type.153
  397.8 104.2 %all-reduce.5.cloned.1.call-done = (bf16[128,4096]{1,0:T(8,128)(2,1)}, bf16[128,4096]{1,0:T(8,128)(2,1)}) async-done(((bf16[128,4096]{1,0:T(8,128)(2,1)}, bf16[128,4096]{1,0:T(8,128)(2,1)}), (bf16[128,4096]{1,0:T(8,128)(2,1)}, bf16[128,4096]{1,0:T(8,128)(2,1)})) %all-reduce.5.cloned.1.call-update) | async-done | bytes 2097168 | tf_op jit(solution)/shard_map/psum | solution.py:117
  502.1 1.7 multiply_reduce_fusion
  (130 shorter events, 27.7 us)
Async XLA Ops:
  7.2 49.0 %copy-start = (bf16[1,4096,128]{2,1,0:T(8,128)(2,1)S(1)}, bf16[1,4096,128]{2,1,0:T(8,128)(2,1)}, u32[]{:S(2)}) copy-start(bf16[1,4096,128]{2,1,0:T(8,128)(2,1)} %param.17) | copy-start | bytes 3145732
  7.2 47.3 %all-gather.14.cloned.1.call-start = ((), (), s32[]{:S(2)}) async-start(), calls=%async_computation.3 | async-start | bytes 1179648 | tf_op jit(solution)/shard_map/all_gather | solution.py:106
  7.9 90.4 %all-gather.16.cloned.1.call-start = ((), (), s32[]{:S(2)}) async-start(), calls=%async_computation.4 | async-start | bytes 1179648 | tf_op jit(solution)/shard_map/all_gather | solution.py:107
  8.7 145.3 %all-gather.10.cloned.1.call-start = ((), (), s32[]{:S(2)}) async-start(), calls=%async_computation.1 | async-start | bytes 2359296 | tf_op jit(solution)/shard_map/all_gather | solution.py:108
  8.7 9.8 %collective-permute-start.1 = (bf16[256,512]{1,0:T(8,128)(2,1)}, bf16[256,512]{1,0:T(8,128)(2,1)S(1)}, u32[]{:S(2)}, u32[]{:S(2)}) collective-permute-start(bf16[256,512]{1,0:T(8,128)(2,1)} %bitcast.282), channel_id=1, source_target_pairs={{0,128},{8,136},{16,144},{24,152},{32,160},{40,168},{48,176},{56,1... | collective-permute-start | bytes 786440 | tf_op jit(solution)/shard_map/ppermute | solution.py:14
  19.3 257.6 %all-reduce.7.cloned.1.call-start = ((), (), s32[]{:S(2)}) async-start(), calls=%async_computation.6 | async-start | bytes 4194304 | tf_op jit(solution)/shard_map/psum | solution.py:117
  19.3 36.8 %copy-start.24 = (f32[1,4096]{1,0:T(1,128)S(1)}, f32[1,4096]{1,0:T(1,128)}, u32[]{:S(2)}) copy-start(f32[1,4096]{1,0:T(1,128)} %param.15) | copy-start | bytes 49156
  54.5 3.4 copy-start.7
  57.9 4.3 copy-start.14
  61.7 2.2 copy-start.1
  155.5 4.2 copy-start.5
  166.9 166.2 %all-gather.12.cloned.1.call-start = ((), (), s32[]{:S(2)}) async-start(), calls=%async_computation.2 | async-start | bytes 1179648 | tf_op jit(solution)/shard_map/all_gather | solution.py:110
  167.5 210.9 %all-gather.8.cloned.1.call-start = ((), (), s32[]{:S(2)}) async-start(), calls=%async_computation | async-start | bytes 1179648 | tf_op jit(solution)/shard_map/all_gather | solution.py:109
  168.1 334.0 %all-reduce.5.cloned.1.call-start = ((), (), s32[]{:S(2)}) async-start(), calls=%async_computation.5 | async-start | bytes 4194304 | tf_op jit(solution)/shard_map/psum | solution.py:117
  276.9 5.8 %copy-start.18 = (bf16[128,4096]{1,0:T(8,128)(2,1)S(1)}, bf16[128,4096]{1,0:T(8,128)(2,1)}, u32[]{:S(2)}) copy-start(bf16[128,4096]{1,0:T(8,128)(2,1)} %get-tuple-element.6) | copy-start | bytes 3145732
  278.9 3.8 copy-start.8
  278.9 9.0 %copy-start.12 = (bf16[512,4096]{1,0:T(8,128)(2,1)S(1)}, bf16[512,4096]{1,0:T(8,128)(2,1)}, u32[]{:S(2)}) copy-start(bf16[512,4096]{1,0:T(8,128)(2,1)} %copy.37) | copy-start | bytes 12582916
  280.8 52.3 %collective-permute-start.2 = (bf16[128,4096]{1,0:T(8,128)(2,1)}, bf16[128,4096]{1,0:T(8,128)(2,1)}, u32[]{:S(2)}, u32[]{:S(2)}) collective-permute-start(bf16[128,4096]{1,0:T(8,128)(2,1)} %fusion.18), channel_id=1, source_target_pairs={{8,0},{16,8},{24,16},{32,24},{40,32},{48,40},{56,48},{64,56},{72,6... | collective-permute-start | bytes 3145736 | tf_op jit(solution)/shard_map/ppermute | solution.py:20
  282.6 8.2 %copy-start.31 = (f32[128]{0:T(128)}, f32[128]{0:T(128)S(1)}, u32[]{:S(2)}) copy-start(f32[128]{0:T(128)S(1)} %get-tuple-element.23) | copy-start | bytes 1540
  283.9 94.5 %collective-permute-start = (bf16[128,4096]{1,0:T(8,128)(2,1)}, bf16[128,4096]{1,0:T(8,128)(2,1)}, u32[]{:S(2)}, u32[]{:S(2)}) collective-permute-start(bf16[128,4096]{1,0:T(8,128)(2,1)} %fusion.11), channel_id=1, source_target_pairs={{0,8},{8,16},{16,24},{24,32},{32,40},{40,48},{48,56},{56,64},{64,7... | collective-permute-start | bytes 3145736 | tf_op jit(solution)/shard_map/ppermute | solution.py:20
  290.8 48.4 %copy-start.28 = (f32[4,128]{1,0:T(4,128)}, f32[4,128]{1,0:T(4,128)S(1)}, u32[]{:S(2)}) copy-start(f32[4,128]{1,0:T(4,128)S(1)} %get-tuple-element.33) | copy-start | bytes 6148
  290.8 48.3 %copy-start.29 = (f32[4,128]{1,0:T(4,128)}, f32[4,128]{1,0:T(4,128)S(1)}, u32[]{:S(2)}) copy-start(f32[4,128]{1,0:T(4,128)S(1)} %fusion.79) | copy-start | bytes 6148
  334.5 4.2 copy-start.6
  334.5 4.8 copy-start.22
  338.7 2.9 copy-start.20
  341.6 38.5 %copy-start.25 = (f32[1,4096]{1,0:T(1,128)S(1)}, f32[1,4096]{1,0:T(1,128)}, u32[]{:S(2)}) copy-start(f32[1,4096]{1,0:T(1,128)} %param.15) | copy-start | bytes 49156
  380.1 4.7 copy-start.9
  380.1 4.7 copy-start.17
  384.3 2.2 copy-start.4
  386.5 2.4 copy-start.2
  392.9 3.4 copy-start.10
  394.4 107.6 %copy-start.26 = (f32[1,4096]{1,0:T(1,128)S(1)}, f32[1,4096]{1,0:T(1,128)}, u32[]{:S(2)}) copy-start(f32[1,4096]{1,0:T(1,128)} %param.15) | copy-start | bytes 49156
  (11 other events, 15.3 us)
Sparse Core Ops, SparseCore 0:
  9.8 44.6 all-gather.13
  56.3 41.9 all-gather.15
  100.7 53.2 all-gather.9
  167.1 109.7 all-reduce.6
  278.5 54.5 all-gather.11
  334.8 43.5 all-gather.7
  393.0 109.0 all-reduce.4
where the time goes:
time: 516 us; the launch traced here: 513 us
  waiting for transfers between devices  413 us (80%)
  matrix products  45.3 us (9%)
  other arithmetic  19.8 us (4%)
  between operations  14.7 us (3%)
  local copies, waits for them, and re-layouts  11.6 us (2%)
  starting transfers between devices  8.83 us (2%)
    psum x2, waiting for transfers between devices, per_device(): lax.psum(partial_value.astype(jnp.bfloat16), 'tensor').astype(jnp.float32)  213 us
    all_gather x1, waiting for transfers between devices, per_device(): lax.all_gather(recalled, 'tensor', axis=1, tiled=True)  51.6 us
    all_gather x1, waiting for transfers between devices, per_device(): lax.all_gather(head_grad, 'tensor', axis=1, tiled=True)  41.8 us
    all_gather x1, waiting for transfers between devices, per_device(): lax.all_gather(new_batch, 'tensor', axis=1, tiled=True)  36.3 us
    all_gather x1, waiting for transfers between devices, per_device(): lax.all_gather(grad_in[0], 'tensor', axis=1, tiled=True)  32.7 us
    all_gather x1, waiting for transfers between devices, per_device(): lax.all_gather(act_in[0], 'tensor', axis=1, tiled=True)  28.7 us
    dot_general x4, matrix products, project_in(): query = jnp.dot(normed, w_query, preferred_element_type=jnp.float32)  13.7 us
  transfers between devices with their start and end apart: 10, of which 8 were waited for; matrix products, arithmetic and copies ran while one was open for 8% of the time, Pallas kernels for 0%

commit v1 on v0

v1 whole, which is shorter than its diff:
```python
import functools

import jax
import jax.numpy as jnp
from jax import lax
from jax.experimental import pallas as pl
from jax.experimental.pallas import tpu as pltpu
from jax.sharding import PartitionSpec as P

HD = 128
EPS = 1e-05
MESH = pl.DeviceIdType.MESH
F32 = jnp.float32
BF16 = jnp.bfloat16

REL = [(0, 0), (0, 1), (1, 0), (3, 0), (1, 1), (3, 1), (2, 0), (2, 1)]


def split_bf16(a):
    hi = a.astype(BF16)
    return hi, (a - hi.astype(F32)).astype(BF16)


def mm3(a, b, dims):
    a_hi, a_lo = split_bf16(a)
    b_hi, b_lo = split_bf16(b)

    def dot(u, w):
        return lax.dot_general(u, w, (dims, ((), ())), preferred_element_type=F32)

    return dot(a_hi, b_hi) + (dot(a_hi, b_lo) + dot(a_lo, b_hi))


NN = ((1,), (0,))
NT = ((1,), (1,))


def heads_to_rows(a):
    return jnp.concatenate([a[:, i : i + HD] for i in range(0, a.shape[1], HD)], axis=0)


def rows_to_heads(a, rows):
    return jnp.concatenate([a[i : i + rows] for i in range(0, a.shape[0], rows)], axis=1)


def softmax_probs(query_rows, keys, rows):
    scores = mm3(query_rows, keys, NT) * HD ** (-0.5)
    row = lax.broadcasted_iota(jnp.int32, (rows, rows), 0)
    col = lax.broadcasted_iota(jnp.int32, (rows, rows), 1)
    causal = jnp.concatenate([row >= col] * (scores.shape[0] // rows), axis=0)
    scores = jnp.where(causal, scores, -1e30)
    expo = jnp.exp(scores - jnp.max(scores, axis=-1, keepdims=True))
    return expo / jnp.sum(expo, axis=-1, keepdims=True)


class Gather:
    def __init__(self, buf, recv, sent, dev):
        self.buf, self.recv, self.sent, self.dev = buf, recv, sent, dev

    def copy(self, src, dst, half, to):
        return pltpu.make_async_remote_copy(
            src_ref=self.buf.at[src, half],
            dst_ref=self.buf.at[dst, half],
            send_sem=self.sent,
            recv_sem=self.recv.at[dst, half],
            device_id=self.dev(*to),
            device_id_type=MESH,
        )

    def wait(self, slot, halves=(0, 1)):
        for half in halves:
            self.copy(slot, slot, half, (0, 1)).wait_recv()

    def start(self):
        for half in range(2):
            self.copy(0, 1, half, (0, 1)).start()
            self.copy(0, 3, half, (1, 0)).start()
            self.copy(0, 2, half, (3, 0)).start()

    def relay_first(self):
        for half in range(2):
            self.wait(1, (half,))
            self.copy(1, 5, half, (1, 0)).start()
            self.copy(1, 4, half, (3, 0)).start()
        self.wait(3, (0,))
        self.copy(3, 6, 0, (1, 0)).start()
        self.wait(2, (1,))
        self.copy(2, 6, 1, (3, 0)).start()

    def relay_second(self):
        for half in range(2):
            self.wait(6, (half,))
            self.copy(6, 7, half, (0, 1)).start()

    def wait_near(self):
        self.wait(3, (1,))
        self.wait(2, (0,))

    def wait_far(self):
        for slot in (4, 5, 7):
            self.wait(slot)

    def drain(self):
        rest = self.buf.at[pl.ds(1, 7)]
        pltpu.make_async_copy(rest, rest, self.sent).wait()


class Scatter:
    def __init__(self, parts, out, got, recv, sent, dev):
        self.parts, self.out, self.got = parts, out, got
        self.recv, self.sent, self.dev = recv, sent, dev
        self.half_rows = out.shape[2]

    def copy(self, slot, half, to):
        return pltpu.make_async_remote_copy(
            src_ref=self.out.at[slot, half],
            dst_ref=self.got.at[slot, half],
            send_sem=self.sent,
            recv_sem=self.recv.at[slot, half],
            device_id=self.dev(*to),
            device_id_type=MESH,
        )

    def wait(self, slot, half):
        self.copy(slot, half, (0, 1)).wait_recv()

    def part(self, slot, half):
        return self.parts[slot, pl.ds(half * self.half_rows, self.half_rows), :]

    def push(self, slot, half, to, adds=()):
        total = self.part(slot, half)
        for other in adds:
            total = total + self.got[other, half].astype(F32)
        self.out[slot, half] = total.astype(BF16)
        self.copy(slot, half, to).start()

    def start_far(self):
        for half in range(2):
            self.push(7, half, (0, 1))
            self.push(4, half, (1, 0))
            self.push(5, half, (3, 0))

    def start_near(self):
        self.push(2, 0, (1, 0))
        self.push(3, 1, (3, 0))

    def relay_first(self):
        for half, to in ((0, (3, 0)), (1, (1, 0))):
            self.wait(7, half)
            self.push(6, half, to, (7,))
        for half in range(2):
            self.wait(4, half)
            self.wait(5, half)
            self.push(1, half, (0, 1), (4, 5))

    def relay_second(self):
        self.wait(6, 0)
        self.push(3, 0, (3, 0), (6,))
        self.wait(6, 1)
        self.push(2, 1, (1, 0), (6,))

    def total(self, half):
        for slot in (1, 2, 3):
            self.wait(slot, half)
        total = self.part(0, half)
        for slot in (1, 2, 3):
            total = total + self.got[slot, half].astype(F32)
        return total

    def drain(self):
        rest = self.out.at[pl.ds(1, 7)]
        pltpu.make_async_copy(rest, rest, self.sent).wait()


def kernel(
    act_ref, grad_ref, stash_ref, fresh_ref, head_ref, gain_ref, wq_ref, wk_ref, wv_ref, wo_ref,
    act_out, grad_out,
    w_in, w_out, gains, ag_first, ag_stash, ag_act, ag_grad,
    parts_f, parts_b, outs, gots, acc_f, acc_s, acc_d, sq_f, sq_s, mixed_ref, dqkv_ref,
    moved_act, moved_grad, sent_act, sent_grad, totals, total_out,
    ag_recv, ag_sent, rs_recv, rs_sent, tot_recv, tot_sent, move_send, move_recv, w_sem,
):
    n_section = lax.axis_size("section")
    section = lax.axis_index("section")
    tensor = lax.axis_index("tensor")
    place_y, place_z = tensor // 2, lax.rem(tensor, 2)
    rows, width = act_ref.shape
    half = rows // 2
    q_cols = wq_ref.shape[2]
    k_cols = wk_ref.shape[2]
    full_width = 8 * width

    def owner(dy, dz):
        return lax.rem(place_y + dy, 4) * 2 + lax.rem(place_z + dz, 2)

    def dev(dy, dz):
        return (section, owner(dy, dz))

    def sec(by):
        return (lax.rem(section + by + n_section, n_section), tensor)

    barrier = pltpu.get_barrier_semaphore()
    for dy, dz in REL[1:]:
        pl.semaphore_signal(barrier, inc=1, device_id=dev(dy, dz), device_id_type=MESH)
    for by in (1, -1, n_section // 2):
        pl.semaphore_signal(barrier, inc=1, device_id=sec(by), device_id_type=MESH)

    loads = []
    for slot, (dy, dz) in enumerate(REL):
        who = owner(dy, dz)
        loads += [
            pltpu.make_async_copy(wq_ref.at[who], w_in.at[slot, :, pl.ds(0, q_cols)], w_sem.at[0]),
            pltpu.make_async_copy(wk_ref.at[who], w_in.at[slot, :, pl.ds(q_cols, k_cols)], w_sem.at[0]),
            pltpu.make_async_copy(wv_ref.at[who], w_in.at[slot, :, pl.ds(q_cols + k_cols, k_cols)], w_sem.at[0]),
            pltpu.make_async_copy(
                wo_ref.at[:, pl.ds(pl.multiple_of(who * width, width), width)], w_out.at[slot], w_sem.at[1]
            ),
        ]
    for load in loads:
        load.start()
    ag_first[0, 0] = act_ref[...]
    ag_first[0, 1] = grad_ref[...]
    pl.semaphore_wait(barrier, 10)

    def move(src, dst, index, by):
        return pltpu.make_async_remote_copy(
            src_ref=src,
            dst_ref=dst,
            send_sem=move_send.at[index],
            recv_sem=move_recv.at[index],
            device_id=sec(by),
            device_id_type=MESH,
        )

    recall = move(stash_ref, ag_stash.at[0], 0, n_section // 2)
    recall.start()
    gather = [
        Gather(buf, ag_recv.at[i], ag_sent.at[i], dev)
        for i, buf in enumerate((ag_first, ag_stash, ag_act, ag_grad))
    ]
    first, stash, act_1, grad_1 = gather
    scatter = [
        Scatter(parts, outs.at[i], gots.at[i], rs_recv.at[i], rs_sent.at[i], dev)
        for i, parts in enumerate((parts_f, parts_b, parts_f, parts_b))
    ]
    first.start()

    for slot, (dy, dz) in enumerate(REL):
        gains[slot] = gain_ref[owner(dy, dz)]
    acc_f[...] = jnp.zeros_like(acc_f)
    acc_s[...] = jnp.zeros_like(acc_s)
    acc_d[...] = jnp.zeros_like(acc_d)
    sq_f[...] = jnp.zeros_like(sq_f)
    sq_s[...] = jnp.zeros_like(sq_s)

    def project(block, slot, acc, squares):
        x = block.astype(F32)
        square = x * x
        squares[...] += sum(square[:, i : i + HD] for i in range(0, width, HD))
        scaled = (x * gains[slot]).astype(BF16)
        acc[...] += jnp.dot(scaled, w_in[slot], preferred_element_type=F32)

    def pull_mixed(block, slot):
        acc_d[...] += lax.dot_general(
            block, w_out[slot], (NT, ((), ())), preferred_element_type=F32
        )

    def inverse_rms(squares):
        mean = jnp.sum(squares, axis=-1, keepdims=True) / full_width
        return lax.rsqrt(mean + EPS)

    def forward_attention():
        inv = inverse_rms(sq_f[...])
        qkv = acc_f[...] * inv
        query = heads_to_rows(qkv[:, :q_cols])
        keys = qkv[:, q_cols : q_cols + k_cols]
        values = qkv[:, q_cols + k_cols :]
        probs = softmax_probs(query, keys, rows)
        mixed_ref[...] = rows_to_heads(mm3(probs, values, NN), rows).astype(BF16)

    def forward_parts(lo, hi):
        @pl.loop(lo, hi)
        def _(slot):
            parts_f[slot] = jnp.dot(mixed_ref[...], w_out[slot], preferred_element_type=F32)

    def backward_parts(lo, hi):
        @pl.loop(lo, hi)
        def _(slot):
            parts_b[slot] = lax.dot_general(
                dqkv_ref[...], w_in[slot], (NT, ((), ())), preferred_element_type=F32
            )

    def diagonal():
        row = lax.broadcasted_iota(jnp.int32, (rows, rows), 0)
        col = lax.broadcasted_iota(jnp.int32, (rows, rows), 1)
        return row == col

    def total_copy(tick, slot, mirror, dy, dz):
        return pltpu.make_async_remote_copy(
            src_ref=total_out.at[tick],
            dst_ref=totals.at[tick, mirror],
            send_sem=tot_sent.at[tick],
            recv_sem=tot_recv.at[tick, mirror],
            device_id=dev(dy, dz),
            device_id_type=MESH,
        )

    def backward_attention(tick):
        at = pl.ds(tick * rows, rows)
        raw = acc_s[at, :]
        qkv = raw * inverse_rms(sq_s[at, :])
        query = heads_to_rows(qkv[:, :q_cols])
        keys = qkv[:, q_cols : q_cols + k_cols]
        values = qkv[:, q_cols + k_cols :]
        probs = softmax_probs(query, keys, rows)
        d_mixed = heads_to_rows(acc_d[...])
        d_values = mm3(probs.T, d_mixed, NN)
        d_probs = mm3(d_mixed, values, NT)
        d_scores = probs * (d_probs - jnp.sum(d_probs * probs, axis=-1, keepdims=True))
        d_scores = d_scores * HD ** (-0.5)
        d_query = rows_to_heads(mm3(d_scores, keys, NN), rows)
        d_keys = mm3(d_scores.T, query, NN)
        dqkv = jnp.concatenate([d_query, d_keys, d_values], axis=1).astype(BF16)
        dqkv_ref[...] = dqkv
        share = jnp.sum(dqkv.astype(F32) * raw, axis=-1, keepdims=True)
        line = jnp.sum(jnp.where(diagonal(), share, 0.0), axis=0, keepdims=True)
        total_out[tick] = jnp.broadcast_to(line, total_out.shape[1:])
        for slot, (dy, dz) in enumerate(REL[1:], 1):
            mirror = REL.index(((4 - dy) % 4, dz))
            total_copy(tick, slot, mirror, dy, dz).start()

    def act_finish(tick, own, rs):
        for i in range(2):
            at = pl.ds(i * half, half)
            out = (own(i).astype(F32) + rs.total(i)).astype(BF16)
            act_out[tick, at, :] = out
            if tick == 0:
                sent_act[at, :] = out

    def grad_finish(tick, own, rs):
        for slot in range(1, 8):
            total_copy(tick, slot, slot, 0, 1).wait_recv()
        line = total_out[tick]
        for slot in range(1, 8):
            line = line + totals[tick, slot]
        full = jnp.where(diagonal(), line[0:1, :], 0.0)
        row_total = jnp.sum(full, axis=-1, keepdims=True)
        inv = inverse_rms(sq_s[pl.ds(tick * rows, rows), :])
        for i in range(2):
            at = pl.ds(i * half, half)
            cut = slice(i * half, (i + 1) * half)
            x = ag_stash[0, tick, at, :].astype(F32)
            scaled = rs.total(i) * gains[0]
            inv_i = inv[cut]
            out = (
                own(i).astype(F32)
                + inv_i * scaled
                - x * (inv_i * inv_i * inv_i) * row_total[cut] / full_width
            ).astype(BF16)
            grad_out[tick, at, :] = out
            if tick == 0:
                sent_grad[at, :] = out

    first.relay_first()
    recall.wait_recv()
    stash.start()
    whole_in, whole_out = w_in.at[...], w_out.at[...]
    pltpu.make_async_copy(whole_in, whole_in, w_sem.at[0]).wait()
    pltpu.make_async_copy(whole_out, whole_out, w_sem.at[1]).wait()
    first.wait_near()

    def first_chunks(lo, hi):
        @pl.loop(lo, hi)
        def _(slot):
            project(ag_first[slot, 0], slot, acc_f, sq_f)
            pull_mixed(ag_first[slot, 1], slot)

    first_chunks(0, 4)
    first.relay_second()
    first.wait_far()
    first_chunks(4, 8)
    forward_attention()
    forward_parts(4, 8)
    scatter[0].start_far()
    forward_parts(0, 4)
    scatter[0].start_near()
    stash.relay_first()
    scatter[0].relay_first()
    stash.wait_near()

    def stash_chunks(lo, hi):
        @pl.loop(lo, hi)
        def _(slot):
            project(ag_stash[slot].reshape(2 * rows, width), slot, acc_s, sq_s)

    stash_chunks(0, 4)
    stash.relay_second()
    scatter[0].relay_second()
    act_finish(0, lambda i: ag_first[0, 0, pl.ds(i * half, half), :], scatter[0])
    shift_act = move(sent_act, moved_act, 1, 1)
    shift_act.start()
    stash.wait_far()
    stash_chunks(4, 8)
    backward_attention(0)
    backward_parts(4, 8)
    scatter[1].start_far()
    backward_parts(0, 4)
    scatter[1].start_near()

    shift_act.wait_recv()
    for i in range(2):
        at = pl.ds(i * half, half)
        ag_act[0, i] = jnp.where(section == 0, fresh_ref[at, :], moved_act[at, :])
    act_1.start()
    scatter[1].relay_first()
    acc_f[...] = jnp.zeros_like(acc_f)
    acc_d[...] = jnp.zeros_like(acc_d)
    sq_f[...] = jnp.zeros_like(sq_f)
    act_1.relay_first()
    scatter[1].relay_second()
    act_1.relay_second()
    grad_finish(0, lambda i: ag_first[0, 1, pl.ds(i * half, half), :], scatter[1])
    shift_grad = move(sent_grad, moved_grad, 2, -1)
    shift_grad.start()
    act_1.wait_near()
    act_1.wait_far()

    @pl.loop(0, 8)
    def _(slot):
        project(ag_act[slot].reshape(rows, width), slot, acc_f, sq_f)

    forward_attention()
    forward_parts(4, 8)
    scatter[2].start_far()
    forward_parts(0, 4)
    scatter[2].start_near()

    shift_grad.wait_recv()
    for i in range(2):
        at = pl.ds(i * half, half)
        ag_grad[0, i] = jnp.where(section == n_section - 1, head_ref[at, :], moved_grad[at, :])
    grad_1.start()
    scatter[2].relay_first()
    grad_1.relay_first()
    scatter[2].relay_second()
    grad_1.relay_second()
    act_finish(1, lambda i: ag_act[0, i], scatter[2])
    grad_1.wait_near()
    grad_1.wait_far()

    @pl.loop(0, 8)
    def _(slot):
        pull_mixed(ag_grad[slot].reshape(rows, width), slot)

    backward_attention(1)
    backward_parts(4, 8)
    scatter[3].start_far()
    backward_parts(0, 4)
    scatter[3].start_near()
    scatter[3].relay_first()
    scatter[3].relay_second()
    grad_finish(1, lambda i: ag_grad[0, i], scatter[3])

    for one in gather + scatter:
        one.drain()
    for tick in range(2):
        rest = totals.at[tick, pl.ds(1, 7)]
        pltpu.make_async_copy(rest, rest, tot_sent.at[tick]).wait()
    for one in (recall, shift_act, shift_grad):
        one.wait_send()


def per_device(
    act_in, grad_in, held_stash, new_batch, head_grad, norm_gain, w_query, w_key, w_value, w_out
):
    rows, width = act_in.shape[1:]
    half = rows // 2
    q_cols, k_cols = w_query.shape[2], w_key.shape[2]
    cols = q_cols + 2 * k_cols
    vmem = pl.BlockSpec(memory_space=pltpu.VMEM)
    hbm = pl.BlockSpec(memory_space=pl.ANY)
    out = jax.ShapeDtypeStruct((2, rows, width), BF16)
    scratch = [
        pltpu.VMEM((8, width, cols), BF16),
        pltpu.VMEM((8, q_cols, width), BF16),
        pltpu.VMEM((8, 1, width), F32),
        pltpu.VMEM((8, 2, rows, width), BF16),
        pltpu.VMEM((8, 2, rows, width), BF16),
        pltpu.VMEM((8, 2, half, width), BF16),
        pltpu.VMEM((8, 2, half, width), BF16),
        pltpu.VMEM((8, rows, width), F32),
        pltpu.VMEM((8, rows, width), F32),
        pltpu.VMEM((4, 8, 2, half, width), BF16),
        pltpu.VMEM((4, 8, 2, half, width), BF16),
        pltpu.VMEM((rows, cols), F32),
        pltpu.VMEM((2 * rows, cols), F32),
        pltpu.VMEM((rows, q_cols), F32),
        pltpu.VMEM((rows, HD), F32),
        pltpu.VMEM((2 * rows, HD), F32),
        pltpu.VMEM((rows, q_cols), BF16),
        pltpu.VMEM((rows, cols), BF16),
        pltpu.VMEM((rows, width), BF16),
        pltpu.VMEM((rows, width), BF16),
        pltpu.VMEM((rows, width), BF16),
        pltpu.VMEM((rows, width), BF16),
        pltpu.VMEM((2, 8, 8, rows), F32),
        pltpu.VMEM((2, 8, rows), F32),
        pltpu.SemaphoreType.DMA((4, 8, 2)),
        pltpu.SemaphoreType.DMA((4,)),
        pltpu.SemaphoreType.DMA((4, 8, 2)),
        pltpu.SemaphoreType.DMA((4,)),
        pltpu.SemaphoreType.DMA((2, 8)),
        pltpu.SemaphoreType.DMA((2,)),
        pltpu.SemaphoreType.DMA((3,)),
        pltpu.SemaphoreType.DMA((3,)),
        pltpu.SemaphoreType.DMA((2,)),
    ]
    acts, grads = pl.pallas_call(
        kernel,
        out_shape=(out, out),
        in_specs=[vmem] * 6 + [hbm] * 4,
        out_specs=(vmem, vmem),
        scratch_shapes=scratch,
        compiler_params=pltpu.CompilerParams(
            collective_id=0, has_side_effects=True, vmem_limit_bytes=52 << 20
        ),
    )(
        act_in[0],
        grad_in[0],
        held_stash[0],
        new_batch,
        head_grad,
        norm_gain.reshape(8, 1, width),
        w_query.reshape(8, width, q_cols),
        w_key.reshape(8, width, k_cols),
        w_value.reshape(8, width, k_cols),
        w_out[0],
    )
    return acts[None], grads[None]


def solution(mesh):
    in_specs = (
        P("section", None, "tensor"),
        P("section", None, "tensor"),
        P("section", None, None, "tensor"),
        P(None, "tensor"),
        P(None, "tensor"),
        P("section", None),
        P("section", None, "tensor"),
        P("section", None, "tensor"),
        P("section", None, "tensor"),
        P("section", "tensor", None),
    )
    out_specs = (P("section", None, None, "tensor"), P("section", None, None, "tensor"))
    return jax.shard_map(
        per_device, mesh=mesh, in_specs=in_specs, out_specs=out_specs, check_vma=False
    )
```

time: 516 us -> 127 us (0.25)
  the two profiles are of different devices: /device:TPU:8 before, /device:TPU:66 now
where the time goes in v1:
time: 127 us; the launch traced here: 126 us
  Pallas kernels  119 us (94%)
  local copies, waits for them, and re-layouts  6.68 us (5%)
    pallas_call x1, Pallas kernels, per_device(): pl.pallas_call(kernel, out_shape=(out, out), in_specs=[vmem] * 6 + [hbm]...  119 us
    unnamed x14, local copies, waits for them, and re-layouts  6.68 us

profile of v1, /device:TPU:66, one launch (start us, length us, event | category | flops | bytes accessed | tf_op | source)
XLA Modules:
  0.0 126.3 jit_solution(96900119589597560)
XLA Ops:
  0.6 0.0 copy-start
  0.6 0.9 copy-done
  1.6 0.0 copy-start.1
  1.6 0.9 copy-done.1
  2.5 0.0 copy-start.2
  2.5 0.9 copy-done.2
  3.4 0.0 copy-start.3
  3.4 0.9 copy-done.3
  4.3 0.0 copy-start.4
  4.3 0.9 copy-done.4
  5.2 0.0 copy-start.5
  5.2 0.7 copy-done.5
  5.9 119.0 %shard_map.113 = (bf16[2,128,512]{2,1,0:T(8,128)(2,1)S(1)}, bf16[2,128,512]{2,1,0:T(8,128)(2,1)S(1)}) custom-call(bf16[128,512]{1,0:T(8,128)(2,1)S(1)} %bitcast.13, bf16[128,512]{1,0:T(8,128)(2,1)S(1)} %bitcast.14, bf16[2,128,512]{2,1,0:T(8,128)(2,1)S(1)} %bitcast.10, bf16[128,512]{1,0:T(8,128)(2,1)S(1)} %copy-done.3, bf16[128,512]{1,0:T(8,128)(2,1)S(1)} %copy-done.4, ...), custom_call_target="tpu_custom_call" | custom-call | tf_op jit(solution)/shard_map/pallas_call | solution.py:518
  124.9 0.7 copy.14
  125.6 0.7 copy.15
Async XLA Ops:
  0.6 1.0 copy-start
  1.6 0.9 copy-start.1
  2.5 0.9 copy-start.2
  3.4 0.9 copy-start.3
  4.3 0.9 copy-start.4
  5.2 0.7 copy-start.5

commit v2 on v1

v2 whole, which is shorter than its diff:
```python
import functools

import jax
import jax.numpy as jnp
from jax import lax
from jax.experimental import pallas as pl
from jax.experimental.pallas import tpu as pltpu
from jax.sharding import PartitionSpec as P

HD = 128
EPS = 1e-05
MESH = pl.DeviceIdType.MESH
F32 = jnp.float32
BF16 = jnp.bfloat16

REL = [(0, 0), (0, 1), (1, 0), (3, 0), (1, 1), (3, 1), (2, 0), (2, 1)]


def split_bf16(a):
    hi = a.astype(BF16)
    return hi, (a - hi.astype(F32)).astype(BF16)


def mm3(a, b, dims):
    a_hi, a_lo = split_bf16(a)
    b_hi, b_lo = split_bf16(b)

    def dot(u, w):
        return lax.dot_general(u, w, (dims, ((), ())), preferred_element_type=F32)

    return dot(a_hi, b_hi) + (dot(a_hi, b_lo) + dot(a_lo, b_hi))


NN = ((1,), (0,))
NT = ((1,), (1,))


def heads_to_rows(a):
    return jnp.concatenate([a[:, i : i + HD] for i in range(0, a.shape[1], HD)], axis=0)


def rows_to_heads(a, rows):
    return jnp.concatenate([a[i : i + rows] for i in range(0, a.shape[0], rows)], axis=1)


def softmax_probs(query_rows, keys, rows):
    scores = mm3(query_rows, keys, NT) * HD ** (-0.5)
    row = lax.broadcasted_iota(jnp.int32, (rows, rows), 0)
    col = lax.broadcasted_iota(jnp.int32, (rows, rows), 1)
    causal = jnp.concatenate([row >= col] * (scores.shape[0] // rows), axis=0)
    scores = jnp.where(causal, scores, -1e30)
    expo = jnp.exp(scores - jnp.max(scores, axis=-1, keepdims=True))
    return expo / jnp.sum(expo, axis=-1, keepdims=True)


class Gather:
    def __init__(self, buf, recv, sent, dev, source, flip):
        self.buf, self.recv, self.sent, self.dev = buf, recv, sent, dev
        self.source, self.flip = source, flip
        self.here = set()

    def copy(self, src, dst, half, to):
        return pltpu.make_async_remote_copy(
            src_ref=self.buf.at[src, half],
            dst_ref=self.buf.at[dst, half],
            send_sem=self.sent,
            recv_sem=self.recv.at[dst, half],
            device_id=self.dev(*to),
            device_id_type=MESH,
        )

    def ready(self, slot, halves=(0, 1)):
        for half in halves:
            if slot and (slot, half) not in self.here:
                self.here.add((slot, half))
                self.copy(slot, slot, half, (0, 1)).wait_recv()

    def start(self, half):
        self.source(self, half)
        self.copy(0, 1, half, (0, 1)).start()
        self.copy(0, 3, half, (1, 0)).start()
        self.copy(0, 2, 1 - half if self.flip else half, (3, 0)).start()

    def across(self, half):
        self.ready(1, (half,))
        self.copy(1, 5, half, (1, 0)).start()
        self.copy(1, 4, half, (3, 0)).start()

    def along_up(self):
        self.ready(3, (0,))
        self.copy(3, 6, 0, (1, 0)).start()

    def along_down(self):
        self.ready(2, (1,))
        self.copy(2, 6, 1, (3, 0)).start()

    def last(self, half):
        self.ready(6, (half,))
        self.copy(6, 7, half, (0, 1)).start()

    def drain(self):
        rest = self.buf.at[pl.ds(1, 7)]
        pltpu.make_async_copy(rest, rest, self.sent).wait()


class Scatter:
    def __init__(self, parts, out, got, recv, sent, dev):
        self.parts, self.out, self.got = parts, out, got
        self.recv, self.sent, self.dev = recv, sent, dev
        self.half_rows = out.shape[2]

    def copy(self, slot, half, to):
        return pltpu.make_async_remote_copy(
            src_ref=self.out.at[slot, half],
            dst_ref=self.got.at[slot, half],
            send_sem=self.sent,
            recv_sem=self.recv.at[slot, half],
            device_id=self.dev(*to),
            device_id_type=MESH,
        )

    def wait(self, slot, half):
        self.copy(slot, half, (0, 1)).wait_recv()

    def part(self, slot, half):
        return self.parts[slot, pl.ds(half * self.half_rows, self.half_rows), :]

    def push(self, slot, half, to, adds=()):
        total = self.part(slot, half)
        for other in adds:
            total = total + self.got[other, half].astype(F32)
        self.out[slot, half] = total.astype(BF16)
        self.copy(slot, half, to).start()

    def begin(self, slot):
        to = {7: (0, 1), 4: (1, 0), 5: (3, 0), 2: (1, 0), 3: (3, 0)}[slot]
        for half in {2: (0,), 3: (1,)}.get(slot, (0, 1)):
            self.push(slot, half, to)

    def last(self, half):
        self.wait(7, half)
        self.push(6, half, (1, 0) if half else (3, 0), (7,))

    def across(self, half):
        self.wait(4, half)
        self.wait(5, half)
        self.push(1, half, (0, 1), (4, 5))

    def along_down(self):
        self.wait(6, 0)
        self.push(3, 0, (3, 0), (6,))

    def along_up(self):
        self.wait(6, 1)
        self.push(2, 1, (1, 0), (6,))

    def total(self, half):
        for slot in (1, 2, 3):
            self.wait(slot, half)
        total = self.part(0, half)
        for slot in (1, 2, 3):
            total = total + self.got[slot, half].astype(F32)
        return total

    def drain(self):
        rest = self.out.at[pl.ds(1, 7)]
        pltpu.make_async_copy(rest, rest, self.sent).wait()


def kernel(
    act_ref, grad_ref, stash_ref, fresh_ref, head_ref, gain_ref, wq_ref, wk_ref, wv_ref, wo_ref,
    act_out, grad_out,
    w_in, w_out, gains, edges, ag, parts_f, parts_b, outs, gots, acc_f, acc_s, acc_d, sq_f, sq_s,
    mixed_ref, dqkv_ref, moved, shifted, totals, total_out,
    ag_recv, ag_sent, rs_recv, rs_sent, tot_recv, tot_sent, recall_send, recall_recv,
    move_send, move_recv, load_sem, w_sem,
):
    n_section = lax.axis_size("section")
    section = lax.axis_index("section")
    tensor = lax.axis_index("tensor")
    place_y, place_z = tensor // 2, lax.rem(tensor, 2)
    half, width = act_ref.shape[1:]
    rows = 2 * half
    q_cols = wq_ref.shape[2]
    k_cols = wk_ref.shape[2]
    full_width = 8 * width

    def owner(dy, dz):
        return lax.rem(place_y + dy, 4) * 2 + lax.rem(place_z + dz, 2)

    def dev(dy, dz):
        return (section, owner(dy, dz))

    def sec(by):
        return (lax.rem(section + by + n_section, n_section), tensor)

    barrier = pltpu.get_barrier_semaphore()
    for dy, dz in REL[1:]:
        pl.semaphore_signal(barrier, inc=1, device_id=dev(dy, dz), device_id_type=MESH)
    for by in (1, -1, n_section // 2):
        pl.semaphore_signal(barrier, inc=1, device_id=sec(by), device_id_type=MESH)

    def own(one, half):
        pass

    def recalled(tick):
        def source(one, half):
            if half == 0:
                recalls[tick].wait_recv()

        return source

    def arrived(index, at_edge):
        def source(one, part):
            shift(index, part, 1).wait_recv()
            edge = edges[index, pl.ds(part * half, half), :]
            one.buf[0, part] = jnp.where(at_edge, edge, moved[index, part])

        return source

    sources = (
        own, own, recalled(0), recalled(1),
        arrived(0, section == 0), arrived(1, section == n_section - 1),
    )
    a0, g0, s0, s1, a1, g1 = [
        Gather(ag.at[i], ag_recv.at[i], ag_sent.at[i], dev, source, i < 4)
        for i, source in enumerate(sources)
    ]
    rs_a0, rs_g0, rs_a1, rs_g1 = [
        Scatter(parts, outs.at[i], gots.at[i], rs_recv.at[i], rs_sent.at[i], dev)
        for i, parts in enumerate((parts_f, parts_b, parts_f, parts_b))
    ]

    loads = [
        pltpu.make_async_copy(act_ref, a0.buf.at[0], load_sem.at[0]),
        pltpu.make_async_copy(grad_ref, g0.buf.at[0], load_sem.at[1]),
    ]
    for slot, (dy, dz) in enumerate(REL):
        loads.append(pltpu.make_async_copy(gain_ref.at[owner(dy, dz)], gains.at[slot], load_sem.at[2]))
    for slot, (dy, dz) in enumerate(REL):
        who = owner(dy, dz)
        loads += [
            pltpu.make_async_copy(wq_ref.at[who], w_in.at[slot, :, pl.ds(0, q_cols)], w_sem.at[0]),
            pltpu.make_async_copy(wk_ref.at[who], w_in.at[slot, :, pl.ds(q_cols, k_cols)], w_sem.at[0]),
            pltpu.make_async_copy(wv_ref.at[who], w_in.at[slot, :, pl.ds(q_cols + k_cols, k_cols)], w_sem.at[0]),
        ]
    for slot, (dy, dz) in enumerate(REL):
        at = pl.ds(pl.multiple_of(owner(dy, dz) * width, width), width)
        loads.append(pltpu.make_async_copy(wo_ref.at[:, at], w_out.at[slot], w_sem.at[1]))
    loads += [
        pltpu.make_async_copy(fresh_ref, edges.at[0], load_sem.at[3]),
        pltpu.make_async_copy(head_ref, edges.at[1], load_sem.at[4]),
    ]
    for load in loads[:10]:
        load.start()
    loads[0].wait()
    loads[1].wait()
    pl.semaphore_wait(barrier, 10)

    recalls = [
        pltpu.make_async_remote_copy(
            src_ref=stash_ref.at[tick],
            dst_ref=one.buf.at[0],
            send_sem=recall_send.at[tick],
            recv_sem=recall_recv.at[tick],
            device_id=sec(n_section // 2),
            device_id_type=MESH,
        )
        for tick, one in enumerate((s0, s1))
    ]

    def shift(index, part, by):
        return pltpu.make_async_remote_copy(
            src_ref=shifted.at[index, part],
            dst_ref=moved.at[index, part],
            send_sem=move_send.at[index, part],
            recv_sem=move_recv.at[index, part],
            device_id=sec(by),
            device_id_type=MESH,
        )

    def clear(*refs):
        for ref in refs:
            ref[...] = jnp.zeros_like(ref)

    def whole(buf, slot):
        return buf[slot].reshape(rows, width)

    def project(one, acc, squares, lo, hi):
        for slot in range(lo, hi):
            one.ready(slot)

        @pl.loop(lo, hi)
        def _(slot):
            x = whole(one.buf, slot).astype(F32)
            square = x * x
            squares[...] += sum(square[:, i : i + HD] for i in range(0, width, HD))
            scaled = (x * gains[slot]).astype(BF16)
            acc[...] += jnp.dot(scaled, w_in[slot], preferred_element_type=F32)

    def pull_mixed(one, lo, hi):
        for slot in range(lo, hi):
            one.ready(slot)

        @pl.loop(lo, hi)
        def _(slot):
            acc_d[...] += lax.dot_general(
                whole(one.buf, slot), w_out[slot], (NT, ((), ())), preferred_element_type=F32
            )

    def inverse_rms(squares):
        mean = jnp.sum(squares, axis=-1, keepdims=True) / full_width
        return lax.rsqrt(mean + EPS)

    def forward_attention():
        qkv = acc_f[...] * inverse_rms(sq_f[...])
        query = heads_to_rows(qkv[:, :q_cols])
        keys = qkv[:, q_cols : q_cols + k_cols]
        values = qkv[:, q_cols + k_cols :]
        probs = softmax_probs(query, keys, rows)
        mixed_ref[...] = rows_to_heads(mm3(probs, values, NN), rows).astype(BF16)

    def forward_parts(lo, hi):
        @pl.loop(lo, hi)
        def _(slot):
            parts_f[slot] = jnp.dot(mixed_ref[...], w_out[slot], preferred_element_type=F32)

    def backward_parts(lo, hi):
        @pl.loop(lo, hi)
        def _(slot):
            parts_b[slot] = lax.dot_general(
                dqkv_ref[...], w_in[slot], (NT, ((), ())), preferred_element_type=F32
            )

    def diagonal():
        row = lax.broadcasted_iota(jnp.int32, (rows, rows), 0)
        col = lax.broadcasted_iota(jnp.int32, (rows, rows), 1)
        return row == col

    def total_copy(tick, mirror, dy, dz):
        return pltpu.make_async_remote_copy(
            src_ref=total_out.at[tick],
            dst_ref=totals.at[tick, mirror],
            send_sem=tot_sent.at[tick],
            recv_sem=tot_recv.at[tick, mirror],
            device_id=dev(dy, dz),
            device_id_type=MESH,
        )

    def backward_attention(tick):
        raw = acc_s[tick]
        qkv = raw * inverse_rms(sq_s[tick])
        query = heads_to_rows(qkv[:, :q_cols])
        keys = qkv[:, q_cols : q_cols + k_cols]
        values = qkv[:, q_cols + k_cols :]
        probs = softmax_probs(query, keys, rows)
        d_mixed = heads_to_rows(acc_d[...])
        d_values = mm3(probs.T, d_mixed, NN)
        d_probs = mm3(d_mixed, values, NT)
        d_scores = probs * (d_probs - jnp.sum(d_probs * probs, axis=-1, keepdims=True))
        d_scores = d_scores * HD ** (-0.5)
        d_query = rows_to_heads(mm3(d_scores, keys, NN), rows)
        d_keys = mm3(d_scores.T, query, NN)
        dqkv = jnp.concatenate([d_query, d_keys, d_values], axis=1).astype(BF16)
        dqkv_ref[...] = dqkv
        share = jnp.sum(dqkv.astype(F32) * raw, axis=-1, keepdims=True)
        line = jnp.sum(jnp.where(diagonal(), share, 0.0), axis=0, keepdims=True)
        total_out[tick] = jnp.broadcast_to(line, total_out.shape[1:])

    def send_totals(tick):
        for dy, dz in REL[1:]:
            total_copy(tick, REL.index(((4 - dy) % 4, dz)), dy, dz).start()

    def act_finish(tick, one, rs, i):
        out = (one.buf[0, i].astype(F32) + rs.total(i)).astype(BF16)
        act_out[tick, pl.ds(i * half, half), :] = out
        if tick == 0:
            shifted[0, i] = out
            shift(0, i, 1).start()

    def grad_finish(tick, one, stashed, rs, i):
        if i == 0:
            for slot in range(1, 8):
                total_copy(tick, slot, 0, 1).wait_recv()
        line = total_out[tick]
        for slot in range(1, 8):
            line = line + totals[tick, slot]
        full = jnp.where(diagonal(), line[0:1, :], 0.0)
        cut = slice(i * half, (i + 1) * half)
        row_total = jnp.sum(full[cut], axis=-1, keepdims=True)
        inv = inverse_rms(sq_s[tick, pl.ds(i * half, half), :])
        x = stashed.buf[0, i].astype(F32)
        scaled = rs.total(i) * gains[0]
        out = (
            one.buf[0, i].astype(F32)
            + inv * scaled
            - x * (inv * inv * inv) * row_total / full_width
        ).astype(BF16)
        grad_out[tick, pl.ds(i * half, half), :] = out
        if tick == 0:
            shifted[1, i] = out
            shift(1, i, -1).start()

    def start_loads():
        for load in loads[10:]:
            load.start()
        recalls[0].start()
        recalls[1].start()

    def wait_weights():
        for buf, sem in ((gains, load_sem.at[2]), (w_in, w_sem.at[0]), (w_out, w_sem.at[1])):
            pltpu.make_async_copy(buf, buf, sem).wait()
        loads[-2].wait()
        loads[-1].wait()

    a0.start(0)
    a0.start(1)
    start_loads()
    clear(acc_f, acc_s, acc_d, sq_f, sq_s)
    g0.start(0)
    g0.start(1)
    a0.along_down()
    a0.along_up()
    wait_weights()
    a0.across(0)
    a0.across(1)
    g0.along_down()
    s0.start(0)
    g0.along_up()
    pull_mixed(g0, 0, 1)
    a0.last(0)
    g0.across(0)
    a0.last(1)
    project(a0, acc_f, sq_f, 0, 1)
    project(a0, acc_f, sq_f, 3, 4)
    s0.start(1)
    s0.along_up()
    g0.last(1)
    pull_mixed(g0, 3, 4)
    project(a0, acc_f, sq_f, 6, 7)
    pull_mixed(g0, 1, 2)
    project(a0, acc_f, sq_f, 4, 5)
    s0.along_down()
    g0.last(0)
    project(a0, acc_f, sq_f, 5, 6)
    project(a0, acc_f, sq_f, 7, 8)
    s0.across(0)
    project(a0, acc_f, sq_f, 1, 3)
    project(s0, acc_s.at[0], sq_s.at[0], 0, 1)
    forward_attention()
    clear(acc_f, sq_f)
    forward_parts(6, 8)
    rs_a0.begin(7)
    project(s0, acc_s.at[0], sq_s.at[0], 1, 2)
    g0.across(1)
    s0.last(1)
    forward_parts(5, 6)
    s0.across(1)
    s0.last(0)
    forward_parts(4, 5)
    rs_a0.begin(4)
    pull_mixed(g0, 2, 3)
    forward_parts(0, 2)
    rs_a0.begin(5)
    rs_a0.last(1)
    pull_mixed(g0, 4, 6)
    s1.start(0)
    rs_a0.last(0)
    s1.start(1)
    forward_parts(2, 4)
    rs_a0.begin(2)
    pull_mixed(g0, 6, 7)
    project(s0, acc_s.at[0], sq_s.at[0], 2, 4)
    rs_a0.across(0)
    project(s0, acc_s.at[0], sq_s.at[0], 4, 5)
    rs_a0.begin(3)
    pull_mixed(g0, 7, 8)
    project(s1, acc_s.at[1], sq_s.at[1], 0, 1)
    project(s0, acc_s.at[0], sq_s.at[0], 7, 8)
    project(s0, acc_s.at[0], sq_s.at[0], 5, 7)
    backward_attention(0)
    backward_parts(7, 8)
    rs_g0.begin(7)
    rs_a0.along_up()
    clear(acc_d)
    rs_a0.along_down()
    backward_parts(4, 5)
    rs_g0.begin(4)
    backward_parts(5, 6)
    rs_g0.begin(5)
    rs_a0.across(1)
    backward_parts(6, 7)
    project(s1, acc_s.at[1], sq_s.at[1], 2, 3)
    rs_g0.last(0)
    rs_g0.last(1)
    act_finish(0, a0, rs_a0, 0)
    act_finish(0, a0, rs_a0, 1)
    s1.across(0)
    backward_parts(1, 2)
    rs_g0.across(0)
    backward_parts(2, 3)
    rs_g0.begin(2)
    backward_parts(0, 1)
    send_totals(0)
    backward_parts(3, 4)
    rs_g0.across(1)
    rs_g0.begin(3)
    rs_g0.along_down()
    rs_g0.along_up()
    a1.start(0)
    a1.start(1)
    grad_finish(0, g0, s0, rs_g0, 0)
    grad_finish(0, g0, s0, rs_g0, 1)
    a1.across(0)
    a1.across(1)
    a1.along_down()
    a1.along_up()
    g1.start(0)
    s1.along_up()
    project(a1, acc_f, sq_f, 0, 1)
    project(a1, acc_f, sq_f, 2, 3)
    g1.start(1)
    pull_mixed(g1, 0, 1)
    project(a1, acc_f, sq_f, 5, 6)
    s1.along_down()
    a1.last(0)
    a1.last(1)
    project(s1, acc_s.at[1], sq_s.at[1], 1, 2)
    project(a1, acc_f, sq_f, 4, 5)
    g1.along_up()
    s1.across(1)
    project(a1, acc_f, sq_f, 6, 7)
    s1.last(0)
    g1.along_down()
    g1.across(0)
    g1.across(1)
    project(a1, acc_f, sq_f, 3, 4)
    s1.last(1)
    pull_mixed(g1, 1, 2)
    pull_mixed(g1, 3, 4)
    project(s1, acc_s.at[1], sq_s.at[1], 3, 4)
    project(a1, acc_f, sq_f, 7, 8)
    g1.last(0)
    project(a1, acc_f, sq_f, 1, 2)
    forward_attention()
    forward_parts(6, 7)
    g1.last(1)
    forward_parts(2, 3)
    rs_a1.begin(2)
    forward_parts(7, 8)
    rs_a1.begin(7)
    project(s1, acc_s.at[1], sq_s.at[1], 4, 5)
    forward_parts(3, 4)
    rs_a1.begin(3)
    project(s1, acc_s.at[1], sq_s.at[1], 5, 6)
    forward_parts(5, 6)
    rs_a1.begin(5)
    project(s1, acc_s.at[1], sq_s.at[1], 7, 8)
    pull_mixed(g1, 6, 7)
    forward_parts(4, 5)
    rs_a1.begin(4)
    project(s1, acc_s.at[1], sq_s.at[1], 6, 7)
    pull_mixed(g1, 2, 3)
    pull_mixed(g1, 4, 6)
    pull_mixed(g1, 7, 8)
    backward_attention(1)
    backward_parts(7, 8)
    rs_g1.begin(7)
    backward_parts(5, 6)
    rs_g1.begin(5)
    forward_parts(0, 1)
    rs_a1.last(1)
    forward_parts(1, 2)
    rs_a1.last(0)
    backward_parts(1, 2)
    backward_parts(4, 5)
    send_totals(1)
    rs_g1.begin(4)
    rs_a1.across(1)
    rs_a1.across(0)
    backward_parts(6, 7)
    rs_g1.last(0)
    rs_g1.last(1)
    backward_parts(0, 1)
    backward_parts(3, 4)
    rs_g1.begin(3)
    rs_a1.along_up()
    rs_g1.across(1)
    rs_g1.across(0)
    backward_parts(2, 3)
    rs_g1.begin(2)
    rs_a1.along_down()
    rs_g1.along_down()
    rs_g1.along_up()
    act_finish(1, a1, rs_a1, 0)
    act_finish(1, a1, rs_a1, 1)
    grad_finish(1, g1, s1, rs_g1, 0)
    grad_finish(1, g1, s1, rs_g1, 1)

    for one in (a0, g0, s0, s1, a1, g1, rs_a0, rs_g0, rs_a1, rs_g1):
        one.drain()
    for tick in range(2):
        rest = totals.at[tick, pl.ds(1, 7)]
        pltpu.make_async_copy(rest, rest, tot_sent.at[tick]).wait()
    for one in recalls:
        one.wait_send()
    for i in range(2):
        shift(0, i, 1).wait_send()
        shift(1, i, -1).wait_send()


def per_device(
    act_in, grad_in, held_stash, new_batch, head_grad, norm_gain, w_query, w_key, w_value, w_out
):
    rows, width = act_in.shape[1:]
    half = rows // 2
    q_cols, k_cols = w_query.shape[2], w_key.shape[2]
    cols = q_cols + 2 * k_cols
    vmem = pl.BlockSpec(memory_space=pltpu.VMEM)
    hbm = pl.BlockSpec(memory_space=pl.ANY)
    out = jax.ShapeDtypeStruct((2, rows, width), BF16)
    scratch = [
        pltpu.VMEM((8, width, cols), BF16),
        pltpu.VMEM((8, q_cols, width), BF16),
        pltpu.VMEM((8, 1, width), F32),
        pltpu.VMEM((2, rows, width), BF16),
        pltpu.VMEM((6, 8, 2, half, width), BF16),
        pltpu.VMEM((8, rows, width), F32),
        pltpu.VMEM((8, rows, width), F32),
        pltpu.VMEM((4, 8, 2, half, width), BF16),
        pltpu.VMEM((4, 8, 2, half, width), BF16),
        pltpu.VMEM((rows, cols), F32),
        pltpu.VMEM((2, rows, cols), F32),
        pltpu.VMEM((rows, q_cols), F32),
        pltpu.VMEM((rows, HD), F32),
        pltpu.VMEM((2, rows, HD), F32),
        pltpu.VMEM((rows, q_cols), BF16),
        pltpu.VMEM((rows, cols), BF16),
        pltpu.VMEM((2, 2, half, width), BF16),
        pltpu.VMEM((2, 2, half, width), BF16),
        pltpu.VMEM((2, 8, 8, rows), F32),
        pltpu.VMEM((2, 8, rows), F32),
        pltpu.SemaphoreType.DMA((6, 8, 2)),
        pltpu.SemaphoreType.DMA((6,)),
        pltpu.SemaphoreType.DMA((4, 8, 2)),
        pltpu.SemaphoreType.DMA((4,)),
        pltpu.SemaphoreType.DMA((2, 8)),
        pltpu.SemaphoreType.DMA((2,)),
        pltpu.SemaphoreType.DMA((2,)),
        pltpu.SemaphoreType.DMA((2,)),
        pltpu.SemaphoreType.DMA((2, 2)),
        pltpu.SemaphoreType.DMA((2, 2)),
        pltpu.SemaphoreType.DMA((5,)),
        pltpu.SemaphoreType.DMA((2,)),
    ]
    acts, grads = pl.pallas_call(
        kernel,
        out_shape=(out, out),
        in_specs=[hbm] * 10,
        out_specs=(vmem, vmem),
        scratch_shapes=scratch,
        compiler_params=pltpu.CompilerParams(
            collective_id=0, has_side_effects=True, vmem_limit_bytes=60 << 20
        ),
    )(
        act_in.reshape(2, half, width),
        grad_in.reshape(2, half, width),
        held_stash.reshape(2, 2, half, width),
        new_batch,
        head_grad,
        norm_gain.reshape(8, 1, width),
        w_query.reshape(8, width, q_cols),
        w_key.reshape(8, width, k_cols),
        w_value.reshape(8, width, k_cols),
        w_out[0],
    )
    return acts[None], grads[None]


def solution(mesh):
    in_specs = (
        P("section", None, "tensor"),
        P("section", None, "tensor"),
        P("section", None, None, "tensor"),
        P(None, "tensor"),
        P(None, "tensor"),
        P("section", None),
        P("section", None, "tensor"),
        P("section", None, "tensor"),
        P("section", None, "tensor"),
        P("section", "tensor", None),
    )
    out_specs = (P("section", None, None, "tensor"), P("section", None, None, "tensor"))
    return jax.shard_map(
        per_device, mesh=mesh, in_specs=in_specs, out_specs=out_specs, check_vma=False
    )
```

time: 127 us -> 91 us (0.72)
  the two profiles are of different devices: /device:TPU:66 before, /device:TPU:8 now
where the time goes in v2:
time: 91 us; the launch traced here: 90.1 us
  Pallas kernels  86.1 us (95%)
  local copies, waits for them, and re-layouts  3.34 us (4%)
    pallas_call x1, Pallas kernels, per_device(): pl.pallas_call(kernel, out_shape=(out, out), in_specs=[hbm] * 10, out_spe...  86.1 us
    unnamed x2, local copies, waits for them, and re-layouts  3.34 us

profile of v2, /device:TPU:8, one launch (start us, length us, event | category | flops | bytes accessed | tf_op | source)
XLA Modules:
  0.0 90.1 jit_solution(13329095066309101647)
XLA Ops:
  0.6 86.1 %shard_map.113 = (bf16[2,128,512]{2,1,0:T(8,128)(2,1)}, bf16[2,128,512]{2,1,0:T(8,128)(2,1)}) custom-call(bf16[2,64,512]{2,1,0:T(8,128)(2,1)} %bitcast.17, bf16[2,64,512]{2,1,0:T(8,128)(2,1)} %bitcast.18, bf16[2,2,64,512]{3,2,1,0:T(8,128)(2,1)} %bitcast.14, bf16[128,512]{1,0:T(8,128)(2,1)} %fresh_ref.1, bf16[128,512]{1,0:T(8,128)(2,1)} %head_ref.1, ...), custom_call_target="tpu_custom_call" | custom-call | tf_op jit(solution)/shard_map/pallas_call | solution.py:656
  86.7 1.7 %copy.14 = bf16[1,2,128,512]{3,2,1,0:T(8,128)(2,1)} copy(bf16[1,2,128,512]{3,2,1,0:T(8,128)(2,1)} %bitcast.16) | data formatting | bytes 524288
  88.4 1.7 %copy.15 = bf16[1,2,128,512]{3,2,1,0:T(8,128)(2,1)} copy(bf16[1,2,128,512]{3,2,1,0:T(8,128)(2,1)} %bitcast.15) | data formatting | bytes 524288

commit v3 on v2

--- a/solution.py
+++ b/solution.py
@@ -13,6 +13,7 @@
 F32 = jnp.float32
 BF16 = jnp.bfloat16
 
+STRIP = 16
 REL = [(0, 0), (0, 1), (1, 0), (3, 0), (1, 1), (3, 1), (2, 0), (2, 1)]
 
 
@@ -54,26 +55,45 @@
 
 
 class Gather:
+    strips = {(5, 0): (3, 0), (4, 1): (2, 1)}
+
     def __init__(self, buf, recv, sent, dev, source, flip):
         self.buf, self.recv, self.sent, self.dev = buf, recv, sent, dev
         self.source, self.flip = source, flip
         self.here = set()
 
     def copy(self, src, dst, half, to):
+        rows = self.buf.shape[2]
+        lo = STRIP if (dst, half) in self.strips else 0
+        at = pl.ds(lo, rows - lo)
         return pltpu.make_async_remote_copy(
-            src_ref=self.buf.at[src, half],
-            dst_ref=self.buf.at[dst, half],
+            src_ref=self.buf.at[src, half, at],
+            dst_ref=self.buf.at[dst, half, at],
             send_sem=self.sent,
             recv_sem=self.recv.at[dst, half],
             device_id=self.dev(*to),
             device_id_type=MESH,
         )
 
+    def strip(self, dst, half):
+        at = pl.ds(0, STRIP)
+        src, _ = self.strips[dst, half]
+        return pltpu.make_async_remote_copy(
+            src_ref=self.buf.at[src, half, at],
+            dst_ref=self.buf.at[dst, half, at],
+            send_sem=self.sent,
+            recv_sem=self.recv.at[0, half],
+            device_id=self.dev(0, 1),
+            device_id_type=MESH,
+        )
+
     def ready(self, slot, halves=(0, 1)):
         for half in halves:
             if slot and (slot, half) not in self.here:
                 self.here.add((slot, half))
                 self.copy(slot, slot, half, (0, 1)).wait_recv()
+                if (slot, half) in self.strips:
+                    self.strip(slot, half).wait_recv()
 
     def start(self, half):
         self.source(self, half)
@@ -89,10 +109,12 @@
     def along_up(self):
         self.ready(3, (0,))
         self.copy(3, 6, 0, (1, 0)).start()
+        self.strip(5, 0).start()
 
     def along_down(self):
         self.ready(2, (1,))
         self.copy(2, 6, 1, (3, 0)).start()
+        self.strip(4, 1).start()
 
     def last(self, half):
         self.ready(6, (half,))
@@ -109,28 +131,45 @@
         self.recv, self.sent, self.dev = recv, sent, dev
         self.half_rows = out.shape[2]
 
-    def copy(self, slot, half, to):
+    def copy(self, slot, half, to, lo=0, hi=None, recv=None):
+        at = pl.ds(lo, (hi or self.half_rows) - lo)
         return pltpu.make_async_remote_copy(
-            src_ref=self.out.at[slot, half],
-            dst_ref=self.got.at[slot, half],
+            src_ref=self.out.at[slot, half, at],
+            dst_ref=self.got.at[slot, half, at],
             send_sem=self.sent,
-            recv_sem=self.recv.at[slot, half],
+            recv_sem=self.recv.at[slot if recv is None else recv, half],
             device_id=self.dev(*to),
             device_id_type=MESH,
         )
 
+    def body(self, slot, half, to):
+        return self.copy(slot, half, to, STRIP if (slot, half) in Gather.strips else 0)
+
+    def strip(self, slot, half):
+        return self.copy(slot, half, (0, 1), 0, STRIP, recv=0)
+
     def wait(self, slot, half):
-        self.copy(slot, half, (0, 1)).wait_recv()
+        self.body(slot, half, (0, 1)).wait_recv()
 
     def part(self, slot, half):
         return self.parts[slot, pl.ds(half * self.half_rows, self.half_rows), :]
 
+    def block(self, slot, half, strip):
+        if strip is None:
+            return self.got[slot, half].astype(F32)
+        lo, hi = (0, STRIP) if strip else (STRIP, self.half_rows)
+        piece = self.got[slot, half, lo:hi].astype(F32)
+        blank = jnp.zeros((self.half_rows - (hi - lo), piece.shape[1]), F32)
+        return jnp.concatenate([piece, blank] if strip else [blank, piece], axis=0)
+
     def push(self, slot, half, to, adds=()):
         total = self.part(slot, half)
-        for other in adds:
-            total = total + self.got[other, half].astype(F32)
+        for other, strip in adds:
+            total = total + self.block(other, half, strip)
         self.out[slot, half] = total.astype(BF16)
-        self.copy(slot, half, to).start()
+        self.body(slot, half, to).start()
+        if (slot, half) in Gather.strips:
+            self.strip(slot, half).start()
 
     def begin(self, slot):
         to = {7: (0, 1), 4: (1, 0), 5: (3, 0), 2: (1, 0), 3: (3, 0)}[slot]
@@ -139,20 +178,22 @@
 
     def last(self, half):
         self.wait(7, half)
-        self.push(6, half, (1, 0) if half else (3, 0), (7,))
+        self.push(6, half, (1, 0) if half else (3, 0), [(7, None)])
 
     def across(self, half):
         self.wait(4, half)
         self.wait(5, half)
-        self.push(1, half, (0, 1), (4, 5))
+        self.push(1, half, (0, 1), [(4, False if half else None), (5, None if half else False)])
 
     def along_down(self):
         self.wait(6, 0)
-        self.push(3, 0, (3, 0), (6,))
+        self.strip(5, 0).wait_recv()
+        self.push(3, 0, (3, 0), [(6, None), (5, True)])
 
     def along_up(self):
         self.wait(6, 1)
-        self.push(2, 1, (1, 0), (6,))
+        self.strip(4, 1).wait_recv()
+        self.push(2, 1, (1, 0), [(6, None), (4, True)])
 
     def total(self, half):
         for slot in (1, 2, 3):
@@ -171,7 +212,7 @@
     act_ref, grad_ref, stash_ref, fresh_ref, head_ref, gain_ref, wq_ref, wk_ref, wv_ref, wo_ref,
     act_out, grad_out,
     w_in, w_out, gains, edges, ag, parts_f, parts_b, outs, gots, acc_f, acc_s, acc_d, sq_f, sq_s,
-    mixed_ref, dqkv_ref, moved, shifted, totals, total_out,
+    mixed_ref, dqkv_ref, moved, totals, total_out,
     ag_recv, ag_sent, rs_recv, rs_sent, tot_recv, tot_sent, recall_send, recall_recv,
     move_send, move_recv, load_sem, w_sem,
 ):
@@ -271,7 +312,7 @@
 
     def shift(index, part, by):
         return pltpu.make_async_remote_copy(
-            src_ref=shifted.at[index, part],
+            src_ref=(act_out, grad_out)[index].at[0, part],
             dst_ref=moved.at[index, part],
             send_sem=move_send.at[index, part],
             recv_sem=move_recv.at[index, part],
@@ -373,9 +414,8 @@
 
     def act_finish(tick, one, rs, i):
         out = (one.buf[0, i].astype(F32) + rs.total(i)).astype(BF16)
-        act_out[tick, pl.ds(i * half, half), :] = out
+        act_out[tick, i] = out
         if tick == 0:
-            shifted[0, i] = out
             shift(0, i, 1).start()
 
     def grad_finish(tick, one, stashed, rs, i):
@@ -396,9 +436,8 @@
             + inv * scaled
             - x * (inv * inv * inv) * row_total / full_width
         ).astype(BF16)
-        grad_out[tick, pl.ds(i * half, half), :] = out
+        grad_out[tick, i] = out
         if tick == 0:
-            shifted[1, i] = out
             shift(1, i, -1).start()
 
     def start_loads():
@@ -416,182 +455,186 @@
     a0.start(0)
     a0.start(1)
     start_loads()
+    g0.start(0)
+    a0.along_up()
+    a0.along_down()
+    s0.start(0)
+    s0.start(1)
+    g0.start(1)
     clear(acc_f, acc_s, acc_d, sq_f, sq_s)
-    g0.start(0)
-    g0.start(1)
-    a0.along_down()
-    a0.along_up()
     wait_weights()
+    pull_mixed(g0, 0, 1)
+    project(a0, acc_f, sq_f, 0, 1)
+    project(s0, acc_s.at[0], sq_s.at[0], 0, 1)
+    g0.along_down()
+    a0.last(0)
+    g0.along_up()
     a0.across(0)
+    s0.along_down()
     a0.across(1)
-    g0.along_down()
-    s0.start(0)
-    g0.along_up()
-    pull_mixed(g0, 0, 1)
-    a0.last(0)
+    a0.last(1)
+    project(a0, acc_f, sq_f, 6, 7)
+    s0.along_up()
+    project(s0, acc_s.at[0], sq_s.at[0], 2, 3)
+    pull_mixed(g0, 1, 2)
+    s0.across(0)
+    s0.across(1)
+    g0.last(0)
+    pull_mixed(g0, 6, 7)
+    pull_mixed(g0, 2, 3)
+    g0.last(1)
+    project(a0, acc_f, sq_f, 2, 4)
     g0.across(0)
-    a0.last(1)
-    project(a0, acc_f, sq_f, 0, 1)
-    project(a0, acc_f, sq_f, 3, 4)
-    s0.start(1)
-    s0.along_up()
-    g0.last(1)
+    project(s0, acc_s.at[0], sq_s.at[0], 1, 2)
+    project(s0, acc_s.at[0], sq_s.at[0], 3, 4)
+    s0.last(1)
     pull_mixed(g0, 3, 4)
-    project(a0, acc_f, sq_f, 6, 7)
-    pull_mixed(g0, 1, 2)
-    project(a0, acc_f, sq_f, 4, 5)
-    s0.along_down()
-    g0.last(0)
-    project(a0, acc_f, sq_f, 5, 6)
     project(a0, acc_f, sq_f, 7, 8)
-    s0.across(0)
-    project(a0, acc_f, sq_f, 1, 3)
-    project(s0, acc_s.at[0], sq_s.at[0], 0, 1)
+    g0.across(1)
+    project(a0, acc_f, sq_f, 1, 2)
+    s0.last(0)
+    project(a0, acc_f, sq_f, 4, 6)
     forward_attention()
     clear(acc_f, sq_f)
-    forward_parts(6, 8)
+    forward_parts(7, 8)
     rs_a0.begin(7)
-    project(s0, acc_s.at[0], sq_s.at[0], 1, 2)
-    g0.across(1)
-    s0.last(1)
-    forward_parts(5, 6)
-    s0.across(1)
-    s0.last(0)
+    s1.start(0)
     forward_parts(4, 5)
     rs_a0.begin(4)
-    pull_mixed(g0, 2, 3)
-    forward_parts(0, 2)
+    forward_parts(5, 6)
     rs_a0.begin(5)
-    rs_a0.last(1)
-    pull_mixed(g0, 4, 6)
-    s1.start(0)
-    rs_a0.last(0)
-    s1.start(1)
-    forward_parts(2, 4)
-    rs_a0.begin(2)
-    pull_mixed(g0, 6, 7)
-    project(s0, acc_s.at[0], sq_s.at[0], 2, 4)
-    rs_a0.across(0)
-    project(s0, acc_s.at[0], sq_s.at[0], 4, 5)
+    forward_parts(6, 7)
+    forward_parts(3, 4)
     rs_a0.begin(3)
     pull_mixed(g0, 7, 8)
+    s1.start(1)
+    project(s0, acc_s.at[0], sq_s.at[0], 6, 7)
+    project(s0, acc_s.at[0], sq_s.at[0], 4, 5)
+    project(s0, acc_s.at[0], sq_s.at[0], 7, 8)
+    pull_mixed(g0, 4, 5)
+    project(s0, acc_s.at[0], sq_s.at[0], 5, 6)
+    pull_mixed(g0, 5, 6)
+    backward_attention(0)
+    send_totals(0)
+    forward_parts(2, 3)
+    rs_a0.last(1)
+    rs_a0.last(0)
+    backward_parts(7, 8)
+    backward_parts(5, 6)
+    rs_g0.begin(7)
+    rs_a0.begin(2)
+    backward_parts(1, 2)
+    rs_g0.begin(5)
+    backward_parts(4, 5)
+    backward_parts(6, 7)
+    rs_g0.begin(4)
+    forward_parts(1, 2)
+    rs_a0.across(1)
     project(s1, acc_s.at[1], sq_s.at[1], 0, 1)
-    project(s0, acc_s.at[0], sq_s.at[0], 7, 8)
-    project(s0, acc_s.at[0], sq_s.at[0], 5, 7)
-    backward_attention(0)
-    backward_parts(7, 8)
-    rs_g0.begin(7)
+    project(s1, acc_s.at[1], sq_s.at[1], 3, 4)
+    rs_g0.last(0)
+    backward_parts(3, 4)
     rs_a0.along_up()
-    clear(acc_d)
     rs_a0.along_down()
-    backward_parts(4, 5)
-    rs_g0.begin(4)
-    backward_parts(5, 6)
-    rs_g0.begin(5)
-    rs_a0.across(1)
-    backward_parts(6, 7)
-    project(s1, acc_s.at[1], sq_s.at[1], 2, 3)
-    rs_g0.last(0)
+    rs_a0.across(0)
     rs_g0.last(1)
-    act_finish(0, a0, rs_a0, 0)
-    act_finish(0, a0, rs_a0, 1)
-    s1.across(0)
-    backward_parts(1, 2)
+    project(s1, acc_s.at[1], sq_s.at[1], 1, 2)
+    s1.along_up()
+    rs_g0.begin(3)
     rs_g0.across(0)
+    rs_g0.across(1)
     backward_parts(2, 3)
     rs_g0.begin(2)
+    rs_g0.along_down()
+    forward_parts(0, 1)
+    act_finish(0, a0, rs_a0, 0)
+    s1.along_down()
     backward_parts(0, 1)
-    send_totals(0)
-    backward_parts(3, 4)
-    rs_g0.across(1)
-    rs_g0.begin(3)
-    rs_g0.along_down()
+    act_finish(0, a0, rs_a0, 1)
     rs_g0.along_up()
+    s1.across(0)
+    s1.across(1)
+    s1.last(0)
+    grad_finish(0, g0, s0, rs_g0, 0)
+    grad_finish(0, g0, s0, rs_g0, 1)
     a1.start(0)
     a1.start(1)
-    grad_finish(0, g0, s0, rs_g0, 0)
-    grad_finish(0, g0, s0, rs_g0, 1)
+    g1.start(0)
+    a1.along_up()
+    g1.start(1)
+    clear(acc_d)
+    pull_mixed(g1, 0, 1)
+    project(s1, acc_s.at[1], sq_s.at[1], 4, 5)
+    a1.along_down()
+    g1.along_up()
+    s1.last(1)
+    project(s1, acc_s.at[1], sq_s.at[1], 6, 7)
     a1.across(0)
+    project(a1, acc_f, sq_f, 0, 1)
+    project(a1, acc_f, sq_f, 2, 4)
+    a1.last(0)
+    g1.along_down()
     a1.across(1)
-    a1.along_down()
-    a1.along_up()
-    g1.start(0)
-    s1.along_up()
-    project(a1, acc_f, sq_f, 0, 1)
-    project(a1, acc_f, sq_f, 2, 3)
-    g1.start(1)
-    pull_mixed(g1, 0, 1)
-    project(a1, acc_f, sq_f, 5, 6)
-    s1.along_down()
-    a1.last(0)
+    pull_mixed(g1, 1, 2)
     a1.last(1)
-    project(s1, acc_s.at[1], sq_s.at[1], 1, 2)
-    project(a1, acc_f, sq_f, 4, 5)
-    g1.along_up()
-    s1.across(1)
-    project(a1, acc_f, sq_f, 6, 7)
-    s1.last(0)
-    g1.along_down()
+    project(s1, acc_s.at[1], sq_s.at[1], 5, 6)
+    pull_mixed(g1, 2, 3)
+    project(a1, acc_f, sq_f, 1, 2)
     g1.across(0)
     g1.across(1)
-    project(a1, acc_f, sq_f, 3, 4)
-    s1.last(1)
-    pull_mixed(g1, 1, 2)
+    project(s1, acc_s.at[1], sq_s.at[1], 7, 8)
+    g1.last(0)
+    project(s1, acc_s.at[1], sq_s.at[1], 2, 3)
+    project(a1, acc_f, sq_f, 6, 7)
     pull_mixed(g1, 3, 4)
-    project(s1, acc_s.at[1], sq_s.at[1], 3, 4)
+    pull_mixed(g1, 6, 7)
+    g1.last(1)
+    project(a1, acc_f, sq_f, 4, 6)
     project(a1, acc_f, sq_f, 7, 8)
-    g1.last(0)
-    project(a1, acc_f, sq_f, 1, 2)
     forward_attention()
-    forward_parts(6, 7)
-    g1.last(1)
+    forward_parts(5, 6)
+    rs_a1.begin(5)
+    forward_parts(4, 5)
+    rs_a1.begin(4)
+    forward_parts(7, 8)
     forward_parts(2, 3)
     rs_a1.begin(2)
-    forward_parts(7, 8)
     rs_a1.begin(7)
-    project(s1, acc_s.at[1], sq_s.at[1], 4, 5)
     forward_parts(3, 4)
+    pull_mixed(g1, 5, 6)
     rs_a1.begin(3)
-    project(s1, acc_s.at[1], sq_s.at[1], 5, 6)
-    forward_parts(5, 6)
-    rs_a1.begin(5)
-    project(s1, acc_s.at[1], sq_s.at[1], 7, 8)
-    pull_mixed(g1, 6, 7)
-    forward_parts(4, 5)
-    rs_a1.begin(4)
-    project(s1, acc_s.at[1], sq_s.at[1], 6, 7)
-    pull_mixed(g1, 2, 3)
-    pull_mixed(g1, 4, 6)
+    pull_mixed(g1, 4, 5)
     pull_mixed(g1, 7, 8)
     backward_attention(1)
     backward_parts(7, 8)
     rs_g1.begin(7)
     backward_parts(5, 6)
     rs_g1.begin(5)
-    forward_parts(0, 1)
+    backward_parts(4, 5)
+    rs_g1.begin(4)
+    forward_parts(6, 7)
+    rs_a1.last(0)
     rs_a1.last(1)
-    forward_parts(1, 2)
-    rs_a1.last(0)
+    backward_parts(0, 1)
+    backward_parts(3, 4)
     backward_parts(1, 2)
-    backward_parts(4, 5)
-    send_totals(1)
-    rs_g1.begin(4)
-    rs_a1.across(1)
-    rs_a1.across(0)
     backward_parts(6, 7)
     rs_g1.last(0)
+    forward_parts(1, 2)
+    rs_a1.across(1)
     rs_g1.last(1)
-    backward_parts(0, 1)
-    backward_parts(3, 4)
-    rs_g1.begin(3)
-    rs_a1.along_up()
-    rs_g1.across(1)
     rs_g1.across(0)
     backward_parts(2, 3)
+    rs_g1.begin(3)
+    rs_g1.across(1)
+    send_totals(1)
     rs_g1.begin(2)
     rs_a1.along_down()
+    rs_a1.across(0)
+    rs_a1.along_up()
     rs_g1.along_down()
     rs_g1.along_up()
+    forward_parts(0, 1)
     act_finish(1, a1, rs_a1, 0)
     act_finish(1, a1, rs_a1, 1)
     grad_finish(1, g1, s1, rs_g1, 0)
@@ -618,7 +661,7 @@
     cols = q_cols + 2 * k_cols
     vmem = pl.BlockSpec(memory_space=pltpu.VMEM)
     hbm = pl.BlockSpec(memory_space=pl.ANY)
-    out = jax.ShapeDtypeStruct((2, rows, width), BF16)
+    out = pltpu.VMEM((2, 2, half, width), BF16)
     scratch = [
         pltpu.VMEM((8, width, cols), BF16),
         pltpu.VMEM((8, q_cols, width), BF16),
@@ -636,7 +679,6 @@
         pltpu.VMEM((2, rows, HD), F32),
         pltpu.VMEM((rows, q_cols), BF16),
         pltpu.VMEM((rows, cols), BF16),
-        pltpu.VMEM((2, 2, half, width), BF16),
         pltpu.VMEM((2, 2, half, width), BF16),
         pltpu.VMEM((2, 8, 8, rows), F32),
         pltpu.VMEM((2, 8, rows), F32),
@@ -674,7 +716,8 @@
         w_value.reshape(8, width, k_cols),
         w_out[0],
     )
-    return acts[None], grads[None]
+    shape = (1, 2, rows, width)
+    return acts.reshape(shape), grads.reshape(shape)
 
 
 def solution(mesh):

time: 91 us -> 86 us (0.945)
  Pallas kernels: 86.1 us -> 83.8 us
  local copies, waits for them, and re-layouts: 3.34 us -> 1.41 us
    pallas_call x1, Pallas kernels: 86.1 us -> 83.8 us  [per_device(): pl.pallas_call(kernel, out_shape=(out, out), in_specs=[hbm] * 10, out_spe...]
    unnamed x2, local copies, waits for them, and re-layouts: 3.34 us -> 1.41 us
where the time goes in v3:
time: 86 us; the launch traced here: 85.9 us
  Pallas kernels  83.8 us (97%)
  local copies, waits for them, and re-layouts  1.41 us (2%)
    pallas_call x1, Pallas kernels, per_device(): pl.pallas_call(kernel, out_shape=(out, out), in_specs=[hbm] * 10, out_spe...  83.8 us

profile of v3, /device:TPU:8, one launch (start us, length us, event | category | flops | bytes accessed | tf_op | source)
XLA Modules:
  0.0 85.9 jit_solution(600689291688889620)
XLA Ops:
  0.6 83.8 %shard_map.113 = (bf16[2,2,64,512]{3,2,1,0:T(8,128)(2,1)S(1)}, bf16[2,2,64,512]{3,2,1,0:T(8,128)(2,1)S(1)}) custom-call(bf16[2,64,512]{2,1,0:T(8,128)(2,1)} %bitcast.17, bf16[2,64,512]{2,1,0:T(8,128)(2,1)} %bitcast.18, bf16[2,2,64,512]{3,2,1,0:T(8,128)(2,1)} %bitcast.16, bf16[128,512]{1,0:T(8,128)(2,1)} %fresh_ref.1, bf16[128,512]{1,0:T(8,128)(2,1)} %head_ref.1, ...), custom_call_target="tpu_custom_call" | custom-call | tf_op jit(solution)/shard_map/pallas_call | solution.py:698
  84.5 0.7 copy.14
  85.2 0.7 copy.15

commit v4 on v3

--- a/solution.py
+++ b/solution.py
@@ -441,10 +441,10 @@
             shift(1, i, -1).start()
 
     def start_loads():
+        recalls[0].start()
+        recalls[1].start()
         for load in loads[10:]:
             load.start()
-        recalls[0].start()
-        recalls[1].start()
 
     def wait_weights():
         for buf, sem in ((gains, load_sem.at[2]), (w_in, w_sem.at[0]), (w_out, w_sem.at[1])):
@@ -456,185 +456,180 @@
     a0.start(1)
     start_loads()
     g0.start(0)
+    g0.start(1)
+    s0.start(0)
+    wait_weights()
     a0.along_up()
     a0.along_down()
-    s0.start(0)
+    g0.along_up()
+    g0.along_down()
     s0.start(1)
-    g0.start(1)
+    s0.along_down()
+    s0.along_up()
     clear(acc_f, acc_s, acc_d, sq_f, sq_s)
-    wait_weights()
-    pull_mixed(g0, 0, 1)
     project(a0, acc_f, sq_f, 0, 1)
-    project(s0, acc_s.at[0], sq_s.at[0], 0, 1)
-    g0.along_down()
     a0.last(0)
-    g0.along_up()
+    a0.last(1)
+    pull_mixed(g0, 0, 2)
+    g0.last(1)
+    project(a0, acc_f, sq_f, 1, 2)
     a0.across(0)
-    s0.along_down()
     a0.across(1)
-    a0.last(1)
+    project(a0, acc_f, sq_f, 3, 4)
+    pull_mixed(g0, 3, 4)
+    g0.across(0)
+    g0.across(1)
+    pull_mixed(g0, 2, 3)
+    g0.last(0)
+    s0.last(0)
+    s0.across(0)
+    s0.last(1)
+    project(a0, acc_f, sq_f, 2, 3)
+    pull_mixed(g0, 6, 7)
+    s0.across(1)
+    project(a0, acc_f, sq_f, 7, 8)
+    project(s0, acc_s.at[0], sq_s.at[0], 0, 2)
     project(a0, acc_f, sq_f, 6, 7)
-    s0.along_up()
-    project(s0, acc_s.at[0], sq_s.at[0], 2, 3)
-    pull_mixed(g0, 1, 2)
-    s0.across(0)
-    s0.across(1)
-    g0.last(0)
-    pull_mixed(g0, 6, 7)
-    pull_mixed(g0, 2, 3)
-    g0.last(1)
-    project(a0, acc_f, sq_f, 2, 4)
-    g0.across(0)
-    project(s0, acc_s.at[0], sq_s.at[0], 1, 2)
-    project(s0, acc_s.at[0], sq_s.at[0], 3, 4)
-    s0.last(1)
-    pull_mixed(g0, 3, 4)
-    project(a0, acc_f, sq_f, 7, 8)
-    g0.across(1)
-    project(a0, acc_f, sq_f, 1, 2)
-    s0.last(0)
     project(a0, acc_f, sq_f, 4, 6)
     forward_attention()
-    clear(acc_f, sq_f)
+    forward_parts(2, 3)
     forward_parts(7, 8)
+    project(s0, acc_s.at[0], sq_s.at[0], 2, 3)
     rs_a0.begin(7)
-    s1.start(0)
     forward_parts(4, 5)
     rs_a0.begin(4)
-    forward_parts(5, 6)
+    s1.start(0)
+    forward_parts(3, 4)
+    project(s0, acc_s.at[0], sq_s.at[0], 6, 7)
+    s1.start(1)
+    pull_mixed(g0, 5, 6)
+    pull_mixed(g0, 7, 8)
+    pull_mixed(g0, 4, 5)
+    forward_parts(1, 2)
+    forward_parts(5, 7)
+    rs_a0.begin(3)
     rs_a0.begin(5)
-    forward_parts(6, 7)
-    forward_parts(3, 4)
-    rs_a0.begin(3)
-    pull_mixed(g0, 7, 8)
-    s1.start(1)
-    project(s0, acc_s.at[0], sq_s.at[0], 6, 7)
-    project(s0, acc_s.at[0], sq_s.at[0], 4, 5)
     project(s0, acc_s.at[0], sq_s.at[0], 7, 8)
-    pull_mixed(g0, 4, 5)
     project(s0, acc_s.at[0], sq_s.at[0], 5, 6)
-    pull_mixed(g0, 5, 6)
+    project(s0, acc_s.at[0], sq_s.at[0], 3, 5)
     backward_attention(0)
     send_totals(0)
-    forward_parts(2, 3)
     rs_a0.last(1)
     rs_a0.last(0)
+    backward_parts(3, 4)
     backward_parts(7, 8)
-    backward_parts(5, 6)
+    forward_parts(0, 1)
+    backward_parts(4, 5)
+    rs_g0.begin(4)
     rs_g0.begin(7)
     rs_a0.begin(2)
+    backward_parts(5, 6)
+    rs_g0.begin(5)
+    rs_a0.across(0)
+    rs_a0.along_up()
+    backward_parts(6, 7)
+    rs_g0.last(0)
+    rs_a0.across(1)
+    rs_a0.along_down()
+    project(s1, acc_s.at[1], sq_s.at[1], 0, 1)
+    rs_g0.last(1)
+    s1.along_up()
+    project(s1, acc_s.at[1], sq_s.at[1], 2, 3)
     backward_parts(1, 2)
-    rs_g0.begin(5)
-    backward_parts(4, 5)
-    backward_parts(6, 7)
-    rs_g0.begin(4)
-    forward_parts(1, 2)
-    rs_a0.across(1)
-    project(s1, acc_s.at[1], sq_s.at[1], 0, 1)
-    project(s1, acc_s.at[1], sq_s.at[1], 3, 4)
-    rs_g0.last(0)
-    backward_parts(3, 4)
-    rs_a0.along_up()
-    rs_a0.along_down()
-    rs_a0.across(0)
-    rs_g0.last(1)
-    project(s1, acc_s.at[1], sq_s.at[1], 1, 2)
-    s1.along_up()
-    rs_g0.begin(3)
-    rs_g0.across(0)
     rs_g0.across(1)
     backward_parts(2, 3)
     rs_g0.begin(2)
+    rs_g0.across(0)
+    rs_g0.begin(3)
     rs_g0.along_down()
-    forward_parts(0, 1)
+    s1.along_down()
+    rs_g0.along_up()
     act_finish(0, a0, rs_a0, 0)
-    s1.along_down()
+    act_finish(0, a0, rs_a0, 1)
     backward_parts(0, 1)
-    act_finish(0, a0, rs_a0, 1)
-    rs_g0.along_up()
+    clear(acc_f, sq_f)
+    s1.last(0)
     s1.across(0)
     s1.across(1)
-    s1.last(0)
     grad_finish(0, g0, s0, rs_g0, 0)
     grad_finish(0, g0, s0, rs_g0, 1)
+    clear(acc_d)
     a1.start(0)
     a1.start(1)
     g1.start(0)
     a1.along_up()
     g1.start(1)
-    clear(acc_d)
+    s1.last(1)
+    project(s1, acc_s.at[1], sq_s.at[1], 3, 4)
+    a1.along_down()
+    project(a1, acc_f, sq_f, 0, 2)
+    g1.along_up()
+    a1.across(0)
+    project(s1, acc_s.at[1], sq_s.at[1], 5, 6)
+    g1.along_down()
+    project(s1, acc_s.at[1], sq_s.at[1], 6, 7)
+    project(a1, acc_f, sq_f, 2, 3)
+    a1.last(0)
+    project(s1, acc_s.at[1], sq_s.at[1], 1, 2)
+    a1.across(1)
+    a1.last(1)
     pull_mixed(g1, 0, 1)
+    pull_mixed(g1, 1, 3)
+    g1.across(0)
+    project(a1, acc_f, sq_f, 3, 4)
+    g1.across(1)
+    g1.last(0)
+    project(a1, acc_f, sq_f, 6, 7)
     project(s1, acc_s.at[1], sq_s.at[1], 4, 5)
-    a1.along_down()
-    g1.along_up()
-    s1.last(1)
-    project(s1, acc_s.at[1], sq_s.at[1], 6, 7)
-    a1.across(0)
-    project(a1, acc_f, sq_f, 0, 1)
-    project(a1, acc_f, sq_f, 2, 4)
-    a1.last(0)
-    g1.along_down()
-    a1.across(1)
-    pull_mixed(g1, 1, 2)
-    a1.last(1)
-    project(s1, acc_s.at[1], sq_s.at[1], 5, 6)
-    pull_mixed(g1, 2, 3)
-    project(a1, acc_f, sq_f, 1, 2)
-    g1.across(0)
-    g1.across(1)
     project(s1, acc_s.at[1], sq_s.at[1], 7, 8)
-    g1.last(0)
-    project(s1, acc_s.at[1], sq_s.at[1], 2, 3)
-    project(a1, acc_f, sq_f, 6, 7)
     pull_mixed(g1, 3, 4)
+    g1.last(1)
     pull_mixed(g1, 6, 7)
-    g1.last(1)
     project(a1, acc_f, sq_f, 4, 6)
     project(a1, acc_f, sq_f, 7, 8)
     forward_attention()
-    forward_parts(5, 6)
-    rs_a1.begin(5)
     forward_parts(4, 5)
     rs_a1.begin(4)
     forward_parts(7, 8)
+    rs_a1.begin(7)
+    forward_parts(5, 6)
+    rs_a1.begin(5)
+    forward_parts(3, 4)
+    rs_a1.begin(3)
     forward_parts(2, 3)
     rs_a1.begin(2)
-    rs_a1.begin(7)
-    forward_parts(3, 4)
-    pull_mixed(g1, 5, 6)
-    rs_a1.begin(3)
-    pull_mixed(g1, 4, 5)
+    pull_mixed(g1, 4, 6)
     pull_mixed(g1, 7, 8)
     backward_attention(1)
+    backward_parts(4, 5)
+    rs_g1.begin(4)
     backward_parts(7, 8)
     rs_g1.begin(7)
+    forward_parts(6, 7)
+    rs_a1.last(0)
     backward_parts(5, 6)
     rs_g1.begin(5)
-    backward_parts(4, 5)
-    rs_g1.begin(4)
-    forward_parts(6, 7)
-    rs_a1.last(0)
+    forward_parts(0, 1)
+    send_totals(1)
     rs_a1.last(1)
+    backward_parts(2, 3)
+    rs_g1.begin(2)
     backward_parts(0, 1)
-    backward_parts(3, 4)
+    backward_parts(6, 7)
     backward_parts(1, 2)
-    backward_parts(6, 7)
-    rs_g1.last(0)
     forward_parts(1, 2)
     rs_a1.across(1)
+    rs_a1.across(0)
+    rs_g1.last(0)
+    backward_parts(3, 4)
+    rs_g1.begin(3)
     rs_g1.last(1)
+    rs_a1.along_up()
+    rs_a1.along_down()
     rs_g1.across(0)
-    backward_parts(2, 3)
-    rs_g1.begin(3)
     rs_g1.across(1)
-    send_totals(1)
-    rs_g1.begin(2)
-    rs_a1.along_down()
-    rs_a1.across(0)
-    rs_a1.along_up()
     rs_g1.along_down()
     rs_g1.along_up()
-    forward_parts(0, 1)
     act_finish(1, a1, rs_a1, 0)
     act_finish(1, a1, rs_a1, 1)
     grad_finish(1, g1, s1, rs_g1, 0)

time: 86 us -> 85.6 us (level)
  no operation moved by 1% of the time
where the time goes in v4:
time: 85.6 us; the launch traced here: 85.4 us
  Pallas kernels  83.4 us (97%)
  local copies, waits for them, and re-layouts  1.41 us (2%)
    pallas_call x1, Pallas kernels, per_device(): pl.pallas_call(kernel, out_shape=(out, out), in_specs=[hbm] * 10, out_spe...  83.4 us

profile of v4, /device:TPU:8, one launch (start us, length us, event | category | flops | bytes accessed | tf_op | source)
XLA Modules:
  0.0 85.4 jit_solution(13140820896716479745)
XLA Ops:
  0.6 83.4 %shard_map.113 = (bf16[2,2,64,512]{3,2,1,0:T(8,128)(2,1)S(1)}, bf16[2,2,64,512]{3,2,1,0:T(8,128)(2,1)S(1)}) custom-call(bf16[2,64,512]{2,1,0:T(8,128)(2,1)} %bitcast.17, bf16[2,64,512]{2,1,0:T(8,128)(2,1)} %bitcast.18, bf16[2,2,64,512]{3,2,1,0:T(8,128)(2,1)} %bitcast.16, bf16[128,512]{1,0:T(8,128)(2,1)} %fresh_ref.1, bf16[128,512]{1,0:T(8,128)(2,1)} %head_ref.1, ...), custom_call_target="tpu_custom_call" | custom-call | tf_op jit(solution)/shard_map/pallas_call | solution.py:693
  84.0 0.7 copy.14
  84.7 0.7 copy.15

commit v5 on v4

--- a/solution.py
+++ b/solution.py
@@ -458,181 +458,178 @@
     g0.start(0)
     g0.start(1)
     s0.start(0)
-    wait_weights()
     a0.along_up()
     a0.along_down()
-    g0.along_up()
     g0.along_down()
+    clear(acc_f, acc_s, acc_d, sq_f, sq_s)
+    wait_weights()
     s0.start(1)
     s0.along_down()
     s0.along_up()
-    clear(acc_f, acc_s, acc_d, sq_f, sq_s)
-    project(a0, acc_f, sq_f, 0, 1)
-    a0.last(0)
+    g0.along_up()
     a0.last(1)
-    pull_mixed(g0, 0, 2)
-    g0.last(1)
-    project(a0, acc_f, sq_f, 1, 2)
+    project(s0, acc_s.at[0], sq_s.at[0], 0, 1)
+    pull_mixed(g0, 0, 1)
+    pull_mixed(g0, 3, 4)
     a0.across(0)
     a0.across(1)
-    project(a0, acc_f, sq_f, 3, 4)
-    pull_mixed(g0, 3, 4)
+    a0.last(0)
+    g0.last(1)
+    g0.last(0)
+    s0.across(0)
+    s0.across(1)
+    project(a0, acc_f, sq_f, 0, 1)
+    s0.last(0)
+    project(a0, acc_f, sq_f, 2, 3)
     g0.across(0)
+    s0.last(1)
+    pull_mixed(g0, 2, 3)
+    project(s0, acc_s.at[0], sq_s.at[0], 3, 4)
+    pull_mixed(g0, 6, 7)
     g0.across(1)
-    pull_mixed(g0, 2, 3)
-    g0.last(0)
-    s0.last(0)
-    s0.across(0)
-    s0.last(1)
-    project(a0, acc_f, sq_f, 2, 3)
-    pull_mixed(g0, 6, 7)
-    s0.across(1)
-    project(a0, acc_f, sq_f, 7, 8)
-    project(s0, acc_s.at[0], sq_s.at[0], 0, 2)
-    project(a0, acc_f, sq_f, 6, 7)
-    project(a0, acc_f, sq_f, 4, 6)
+    project(s0, acc_s.at[0], sq_s.at[0], 2, 3)
+    pull_mixed(g0, 1, 2)
+    project(a0, acc_f, sq_f, 6, 8)
+    project(a0, acc_f, sq_f, 1, 2)
+    project(a0, acc_f, sq_f, 3, 6)
     forward_attention()
-    forward_parts(2, 3)
-    forward_parts(7, 8)
-    project(s0, acc_s.at[0], sq_s.at[0], 2, 3)
+    forward_parts(5, 8)
     rs_a0.begin(7)
+    rs_a0.begin(5)
     forward_parts(4, 5)
     rs_a0.begin(4)
+    project(s0, acc_s.at[0], sq_s.at[0], 4, 5)
+    forward_parts(0, 1)
+    project(s0, acc_s.at[0], sq_s.at[0], 1, 2)
+    forward_parts(2, 3)
+    pull_mixed(g0, 7, 8)
+    forward_parts(3, 4)
     s1.start(0)
-    forward_parts(3, 4)
-    project(s0, acc_s.at[0], sq_s.at[0], 6, 7)
     s1.start(1)
-    pull_mixed(g0, 5, 6)
-    pull_mixed(g0, 7, 8)
-    pull_mixed(g0, 4, 5)
-    forward_parts(1, 2)
-    forward_parts(5, 7)
-    rs_a0.begin(3)
-    rs_a0.begin(5)
+    project(s1, acc_s.at[1], sq_s.at[1], 0, 1)
+    pull_mixed(g0, 4, 6)
+    project(s0, acc_s.at[0], sq_s.at[0], 5, 7)
     project(s0, acc_s.at[0], sq_s.at[0], 7, 8)
-    project(s0, acc_s.at[0], sq_s.at[0], 5, 6)
-    project(s0, acc_s.at[0], sq_s.at[0], 3, 5)
     backward_attention(0)
-    send_totals(0)
+    rs_a0.last(0)
     rs_a0.last(1)
-    rs_a0.last(0)
-    backward_parts(3, 4)
-    backward_parts(7, 8)
-    forward_parts(0, 1)
+    backward_parts(0, 1)
+    rs_a0.begin(2)
     backward_parts(4, 5)
     rs_g0.begin(4)
+    rs_a0.begin(3)
+    backward_parts(6, 8)
     rs_g0.begin(7)
-    rs_a0.begin(2)
     backward_parts(5, 6)
+    send_totals(0)
     rs_g0.begin(5)
+    rs_a0.along_up()
+    forward_parts(1, 2)
+    rs_a0.across(1)
+    rs_g0.last(0)
     rs_a0.across(0)
-    rs_a0.along_up()
-    backward_parts(6, 7)
-    rs_g0.last(0)
-    rs_a0.across(1)
-    rs_a0.along_down()
-    project(s1, acc_s.at[1], sq_s.at[1], 0, 1)
+    backward_parts(2, 3)
     rs_g0.last(1)
     s1.along_up()
-    project(s1, acc_s.at[1], sq_s.at[1], 2, 3)
+    rs_a0.along_down()
     backward_parts(1, 2)
+    rs_g0.across(0)
     rs_g0.across(1)
-    backward_parts(2, 3)
-    rs_g0.begin(2)
-    rs_g0.across(0)
+    backward_parts(3, 4)
     rs_g0.begin(3)
     rs_g0.along_down()
     s1.along_down()
+    rs_g0.begin(2)
     rs_g0.along_up()
+    s1.across(0)
     act_finish(0, a0, rs_a0, 0)
+    s1.across(1)
     act_finish(0, a0, rs_a0, 1)
-    backward_parts(0, 1)
+    s1.last(0)
     clear(acc_f, sq_f)
-    s1.last(0)
-    s1.across(0)
-    s1.across(1)
     grad_finish(0, g0, s0, rs_g0, 0)
     grad_finish(0, g0, s0, rs_g0, 1)
-    clear(acc_d)
     a1.start(0)
     a1.start(1)
     g1.start(0)
     a1.along_up()
+    s1.last(1)
+    clear(acc_d)
     g1.start(1)
-    s1.last(1)
-    project(s1, acc_s.at[1], sq_s.at[1], 3, 4)
+    project(a1, acc_f, sq_f, 0, 1)
+    project(s1, acc_s.at[1], sq_s.at[1], 1, 2)
+    project(a1, acc_f, sq_f, 3, 4)
     a1.along_down()
-    project(a1, acc_f, sq_f, 0, 2)
+    project(a1, acc_f, sq_f, 1, 2)
+    project(s1, acc_s.at[1], sq_s.at[1], 5, 6)
     g1.along_up()
     a1.across(0)
-    project(s1, acc_s.at[1], sq_s.at[1], 5, 6)
+    a1.last(0)
     g1.along_down()
-    project(s1, acc_s.at[1], sq_s.at[1], 6, 7)
-    project(a1, acc_f, sq_f, 2, 3)
-    a1.last(0)
-    project(s1, acc_s.at[1], sq_s.at[1], 1, 2)
     a1.across(1)
     a1.last(1)
-    pull_mixed(g1, 0, 1)
-    pull_mixed(g1, 1, 3)
     g1.across(0)
-    project(a1, acc_f, sq_f, 3, 4)
+    project(a1, acc_f, sq_f, 6, 7)
     g1.across(1)
+    project(a1, acc_f, sq_f, 2, 3)
+    pull_mixed(g1, 0, 3)
+    project(s1, acc_s.at[1], sq_s.at[1], 6, 7)
     g1.last(0)
-    project(a1, acc_f, sq_f, 6, 7)
+    pull_mixed(g1, 3, 4)
+    project(s1, acc_s.at[1], sq_s.at[1], 2, 3)
     project(s1, acc_s.at[1], sq_s.at[1], 4, 5)
+    pull_mixed(g1, 6, 7)
     project(s1, acc_s.at[1], sq_s.at[1], 7, 8)
-    pull_mixed(g1, 3, 4)
     g1.last(1)
-    pull_mixed(g1, 6, 7)
+    project(s1, acc_s.at[1], sq_s.at[1], 3, 4)
     project(a1, acc_f, sq_f, 4, 6)
     project(a1, acc_f, sq_f, 7, 8)
     forward_attention()
     forward_parts(4, 5)
     rs_a1.begin(4)
+    forward_parts(5, 6)
+    rs_a1.begin(5)
     forward_parts(7, 8)
     rs_a1.begin(7)
-    forward_parts(5, 6)
-    rs_a1.begin(5)
+    forward_parts(2, 3)
+    rs_a1.begin(2)
     forward_parts(3, 4)
     rs_a1.begin(3)
-    forward_parts(2, 3)
-    rs_a1.begin(2)
     pull_mixed(g1, 4, 6)
     pull_mixed(g1, 7, 8)
     backward_attention(1)
+    backward_parts(7, 8)
+    rs_g1.begin(7)
     backward_parts(4, 5)
     rs_g1.begin(4)
-    backward_parts(7, 8)
-    rs_g1.begin(7)
-    forward_parts(6, 7)
-    rs_a1.last(0)
     backward_parts(5, 6)
     rs_g1.begin(5)
-    forward_parts(0, 1)
-    send_totals(1)
-    rs_a1.last(1)
-    backward_parts(2, 3)
-    rs_g1.begin(2)
-    backward_parts(0, 1)
-    backward_parts(6, 7)
-    backward_parts(1, 2)
+    forward_parts(6, 7)
     forward_parts(1, 2)
     rs_a1.across(1)
     rs_a1.across(0)
+    rs_a1.last(1)
+    rs_a1.last(0)
+    backward_parts(2, 3)
+    rs_g1.begin(2)
+    backward_parts(3, 4)
+    backward_parts(6, 7)
     rs_g1.last(0)
-    backward_parts(3, 4)
+    rs_g1.last(1)
     rs_g1.begin(3)
-    rs_g1.last(1)
+    backward_parts(1, 2)
+    send_totals(1)
+    forward_parts(0, 1)
+    rs_a1.along_down()
     rs_a1.along_up()
-    rs_a1.along_down()
+    rs_g1.across(1)
+    backward_parts(0, 1)
+    rs_g1.along_down()
     rs_g1.across(0)
-    rs_g1.across(1)
-    rs_g1.along_down()
     rs_g1.along_up()
     act_finish(1, a1, rs_a1, 0)
+    grad_finish(1, g1, s1, rs_g1, 0)
     act_finish(1, a1, rs_a1, 1)
-    grad_finish(1, g1, s1, rs_g1, 0)
     grad_finish(1, g1, s1, rs_g1, 1)
 
     for one in (a0, g0, s0, s1, a1, g1, rs_a0, rs_g0, rs_a1, rs_g1):

time: 85.6 us -> 87.8 us (1.026)
  Pallas kernels: 83.4 us -> 85.6 us
    pallas_call x1, Pallas kernels: 83.4 us -> 85.6 us  [per_device(): pl.pallas_call(kernel, out_shape=(out, out), in_specs=[hbm] * 10, out_spe...]
where the time goes in v5:
time: 87.8 us; the launch traced here: 87.7 us
  Pallas kernels  85.6 us (97%)
  local copies, waits for them, and re-layouts  1.41 us (2%)
    pallas_call x1, Pallas kernels, per_device(): pl.pallas_call(kernel, out_shape=(out, out), in_specs=[hbm] * 10, out_spe...  85.6 us

profile of v5, /device:TPU:8, one launch (start us, length us, event | category | flops | bytes accessed | tf_op | source)
XLA Modules:
  0.0 87.7 jit_solution(12681351352962978047)
XLA Ops:
  0.6 85.6 %shard_map.113 = (bf16[2,2,64,512]{3,2,1,0:T(8,128)(2,1)S(1)}, bf16[2,2,64,512]{3,2,1,0:T(8,128)(2,1)S(1)}) custom-call(bf16[2,64,512]{2,1,0:T(8,128)(2,1)} %bitcast.17, bf16[2,64,512]{2,1,0:T(8,128)(2,1)} %bitcast.18, bf16[2,2,64,512]{3,2,1,0:T(8,128)(2,1)} %bitcast.16, bf16[128,512]{1,0:T(8,128)(2,1)} %fresh_ref.1, bf16[128,512]{1,0:T(8,128)(2,1)} %head_ref.1, ...), custom_call_target="tpu_custom_call" | custom-call | tf_op jit(solution)/shard_map/pallas_call | solution.py:690
  86.2 0.7 copy.14
  87.0 0.7 copy.15
